TPU v7x, 512 devices: a whole 4x4x16 slice. The times are simulated.
512 devices in a mesh: les: 128 (over z, x, y_hi), cnn: 4 (over y_lo, core).
Axes of the slice: x: 4, y: 4 (y_hi: 2, y_lo: 2; y = y_hi * 2 + y_lo), z: 16, core: 2. Of those that a mesh axis runs over, the one named last changes fastest.
Arguments:
- velocity: float32 [3, 256, 256, 512], P(None, 'les', None, 'cnn'), may hold values from -6 to 6
- target_stress: bfloat16 [2, 256, 512, 2], P(None, 'les', 'cnn'), may hold values from -6 to 6
- owner_map: int32 [32768, 1], P(('les', 'cnn')), may hold values from 0 to 127; in each aligned block of 64 rows (0 to 63, 64 to 127, ...) at most 2 rows name the same one
- train_order: int32 [512, 64], P(('les', 'cnn')), may hold values from 0 to 63, each once within a row
- w_first: bfloat16 [128, 432, 128], P('les'), may hold values from -0.3125 to 0.3125
- w_mid: bfloat16 [128, 1152, 128], P('les'), may hold values from -0.1875 to 0.1875
- w_out: bfloat16 [128, 128, 2], P('les'), may hold values from -0.5 to 0.5
Outputs:
- new_velocity: float32 [3, 256, 256, 512], P(None, 'les', None, 'cnn')
- wall_stress: float32 [2, 256, 512, 2], P(None, 'les', 'cnn')
- grad_first: float32 [128, 432, 128], P('les')
- grad_mid: float32 [128, 1152, 128], P('les')
- grad_out: float32 [128, 128, 2], P('les')
Inputs may be any that keep to these rules, and one draw needn't show every extreme that they name: `owner_map`: among the tiles of one device at most 2 name the same expert, a bound that some block reaches of them. `train_order`: each row holds every rank once.
All inputs are finite; a program needn't handle non-finite values.
Results may differ from a plain program's by a relative error of at most 0.005.
Values may be sent and summed in bfloat16 or wider, within the bound.
A program may use at most 64 MiB of HBM per device.

v0:
```python
import math

import jax
import jax.numpy as jnp
from jax import lax
from jax.sharding import PartitionSpec as P

TX = 4
NPL = 16


DT_STEP = 0.25
VISCOSITY = 0.05
FORCING = 0.2


def extended(value, sides, width):
    for axis, dim in sides:
        size, length = (lax.axis_size(axis), value.shape[dim])
        up = [(i, (i + 1) % size) for i in range(size)]
        down = [(j, i) for i, j in up]
        last = lax.slice_in_dim(value, length - width, length, axis=dim)
        initial = lax.slice_in_dim(value, 0, width, axis=dim)
        before = lax.ppermute(last, axis, up)
        after = lax.ppermute(initial, axis, down)
        value = jnp.concatenate([before, value, after], axis=dim)
    return value


def patches(values, mirror):
    height = values.shape[1]
    breadth = values.shape[2]
    padded = jnp.pad(values, ((0, 0), (1, 1), (1, 1), (0, 0)))
    pieces = []
    for shift_z in (-1, 0, 1):
        for shift_x in (-1, 0, 1):
            start_z = 1 + mirror * shift_z
            start_x = 1 + mirror * shift_x
            pieces.append(padded[:, start_z : start_z + height, start_x : start_x + breadth, :])
    return jnp.concatenate(pieces, axis=3)


def silu_slope(values):
    logistic = jax.nn.sigmoid(values)
    return logistic * (1.0 + values * (1.0 - logistic))


def tendency(padded):
    center = padded[:, 1:-1, :, 1:-1]
    mirror = jnp.array([1.0, -1.0, 1.0], dtype=center.dtype)[:, None, None, None]
    column = jnp.concatenate(
        [center[:, :, :1, :] * mirror, center, center[:, :, -1:, :] * mirror], axis=2
    )
    x_plus = padded[:, 1:-1, :, 2:]
    x_minus = padded[:, 1:-1, :, :-2]
    z_plus = padded[:, 2:, :, 1:-1]
    z_minus = padded[:, :-2, :, 1:-1]
    y_plus = column[:, :, 2:, :]
    y_minus = column[:, :, :-2, :]
    advect = 0.5 * (
        center[0:1] * (x_plus - x_minus)
        + center[1:2] * (y_plus - y_minus)
        + center[2:3] * (z_plus - z_minus)
    )
    laplace = x_plus + x_minus + z_plus + z_minus + y_plus + y_minus - 6.0 * center
    forcing_term = jnp.array([FORCING, 0.0, 0.0], dtype=center.dtype)[:, None, None, None]
    return VISCOSITY * laplace - advect + forcing_term


def wall_term(values, stress, factor):
    values = values.at[0, :, 0, :].add(factor * stress[0, :, :, 0])
    values = values.at[2, :, 0, :].add(factor * stress[0, :, :, 1])
    values = values.at[0, :, -1, :].add(factor * stress[1, :, :, 0])
    values = values.at[2, :, -1, :].add(factor * stress[1, :, :, 1])
    return values


def surround(velocity):
    return extended(velocity, (("les", 1), ("cnn", 3)), 1)


def expert_pass(tile_data, tile_targets, train_mask, w_one, w_two, w_three, loss_scale):
    flt = jnp.float32
    first_cols = patches(tile_data, 1)
    pre_one = jnp.einsum("sztk,kc->sztc", first_cols, w_one, preferred_element_type=flt)
    hidden_one = jax.nn.silu(pre_one).astype(jnp.bfloat16)
    middle = patches(hidden_one, 1)
    pre_two = jnp.einsum("sztk,kc->sztc", middle, w_two, preferred_element_type=flt)
    hidden_two = (jax.nn.silu(pre_two) + hidden_one.astype(flt)).astype(jnp.bfloat16)
    predicted = jnp.einsum("sztc,co->szto", hidden_two, w_three, preferred_element_type=flt)
    error_term = (
        2.0
        * loss_scale
        * train_mask.astype(flt)[:, None, None, None]
        * (predicted - tile_targets.astype(flt))
    ).astype(jnp.bfloat16)
    grad_three = jnp.einsum("sztc,szto->co", hidden_two, error_term, preferred_element_type=flt)
    grad_two_h = jnp.einsum("szto,co->sztc", error_term, w_three, preferred_element_type=flt)
    grad_pre_two = (grad_two_h * silu_slope(pre_two)).astype(jnp.bfloat16)
    grad_two = jnp.einsum("sztk,sztc->kc", middle, grad_pre_two, preferred_element_type=flt)
    chans = w_two.shape[1]
    turned = w_two.reshape(9, chans, chans).transpose(0, 2, 1).reshape(9 * chans, chans)
    grad_one_h = grad_two_h + jnp.einsum(
        "sztk,kc->sztc", patches(grad_pre_two, -1), turned, preferred_element_type=flt
    )
    grad_pre_one = (grad_one_h * silu_slope(pre_one)).astype(jnp.bfloat16)
    grad_one = jnp.einsum("sztk,sztc->kc", first_cols, grad_pre_one, preferred_element_type=flt)
    return (predicted, (grad_one, grad_two, grad_three))


def wall_models(velocity, target_stress, owner_map, train_order, w_first, w_mid, w_out):
    owners_count = lax.axis_size("les")
    tile_count = owner_map.shape[0]
    capacity = max(2, 2 * tile_count // owners_count)
    slots_total = owners_count * capacity
    depth = velocity.shape[1]
    breadth = velocity.shape[3]
    tiles_along = breadth // TX
    loss_scale = 1.0 / math.sqrt(TX * depth * tile_count * lax.axis_size("cnn"))
    mirror = jnp.array([1.0, -1.0, 1.0], dtype=jnp.float32)[:, None, None, None]
    bottom = velocity[:, :, :NPL, :]
    top = jnp.flip(velocity, axis=2)[:, :, :NPL, :] * mirror
    walls = jnp.stack([bottom, top]).reshape(2, 3, depth, NPL, tiles_along, TX)
    tile_data = walls.transpose(0, 4, 2, 5, 1, 3).reshape(tile_count, -1).astype(jnp.bfloat16)
    tile_targets = (
        target_stress.reshape(2, depth, tiles_along, TX, 2)
        .transpose(0, 2, 1, 3, 4)
        .reshape(tile_count, -1)
    )
    train_mask = (train_order[0] < tile_count // 2).astype(jnp.bfloat16)
    owners = owner_map[:, 0]
    same_owner = owners[:, None] == owners[None, :]
    positions = jnp.arange(tile_count)
    earlier = positions[None, :] < positions[:, None]
    rank_in = jnp.sum(jnp.logical_and(same_owner, earlier), axis=1)
    slot_index = owners * capacity + rank_in
    send_data = (
        jnp.zeros((slots_total, tile_data.shape[1]), jnp.bfloat16)
        .at[slot_index]
        .set(tile_data)
        .reshape(owners_count, capacity, -1)
    )
    send_targets = (
        jnp.zeros((slots_total, tile_targets.shape[1]), jnp.bfloat16)
        .at[slot_index]
        .set(tile_targets)
        .reshape(owners_count, capacity, -1)
    )
    send_mask = (
        jnp.zeros((slots_total,), jnp.bfloat16)
        .at[slot_index]
        .set(train_mask)
        .reshape(owners_count, capacity)
    )
    got_data, got_targets, got_mask = (
        lax.all_to_all(send_data, "les", split_axis=0, concat_axis=0, tiled=True),
        lax.all_to_all(send_targets, "les", split_axis=0, concat_axis=0, tiled=True),
        lax.all_to_all(send_mask, "les", split_axis=0, concat_axis=0, tiled=True),
    )
    predicted, grads = expert_pass(
        got_data.reshape(slots_total, depth, TX, 3 * NPL),
        got_targets.reshape(slots_total, depth, TX, 2),
        got_mask.reshape(slots_total),
        w_first[0],
        w_mid[0],
        w_out[0],
        loss_scale,
    )
    returned = lax.all_to_all(
        predicted.reshape(owners_count, capacity, -1),
        "les",
        split_axis=0,
        concat_axis=0,
        tiled=True,
    )
    own_stress = returned.reshape(slots_total, -1)[slot_index]
    stress = (
        own_stress.reshape(2, tiles_along, depth, TX, 2)
        .transpose(0, 2, 1, 3, 4)
        .reshape(2, depth, breadth, 2)
    )
    return (stress, grads)


def per_device(velocity, target_stress, owner_map, train_order, w_first, w_mid, w_out):
    stress, grads = wall_models(
        velocity, target_stress, owner_map, train_order, w_first, w_mid, w_out
    )
    change = wall_term(tendency(surround(velocity)), stress, -1.0)
    new_velocity = velocity + DT_STEP * change
    summed = lax.psum((grads[0], grads[1], grads[2]), "cnn")
    return (new_velocity, stress, summed[0][None], summed[1][None], summed[2][None])


def solution(mesh):
    placed = (
        P(None, "les", None, "cnn"),
        P(None, "les", "cnn", None),
        P(("les", "cnn"), None),
        P(("les", "cnn"), None),
        P("les", None, None),
        P("les", None, None),
        P("les", None, None),
    )
    return jax.shard_map(
        per_device,
        mesh=mesh,
        in_specs=placed,
        out_specs=(
            P(None, "les", None, "cnn"),
            P(None, "les", "cnn", None),
            P("les", None, None),
            P("les", None, None),
            P("les", None, None),
        ),
        check_vma=False,
    )
```

profile of v0, /device:TPU:1, one launch (start us, length us, event | category | flops | bytes accessed | tf_op | source)
XLA Modules:
  0.0 224.7 jit_solution(9193366580393969351)
XLA Ops:
  7.2 0.9 convert_reduce_fusion
  8.1 0.7 fusion.50
  8.8 0.7 fusion.49
  9.5 1.0 scatter_custom_fusion.1
  10.4 0.8 all_to_all.20
  11.2 23.0 %all-to-all-start.2 = ((bf16[128,1,2]{2,1,0:T(2,128)(2,1)}), bf16[128,1,2]{2,1,0:T(2,128)(2,1)S(1)}, u32[]{:S(2)}, u32[]{:S(2)}) async-start(bf16[128,1,2]{2,1,0:T(2,128)(2,1)} %all_to_all.20), calls=%async_computation.2 | async-start | bytes 131072 | tf_op jit(solution)/shard_map/all_to_all | solution.py:158
  34.2 1.9 fusion.58
  36.1 4.0 %collective-permute-start = (f32[3,1,256,128]{3,2,1,0:T(8,128)S(1)}, f32[3,1,256,128]{3,2,1,0:T(8,128)S(1)}, u32[]{:S(2)}, u32[]{:S(2)}) collective-permute-start(f32[3,1,256,128]{3,2,1,0:T(8,128)S(1)} %get-tuple-element.88), channel_id=1, source_target_pairs={{0,4},{4,8},{8,12},{12,16},{16,20},{20,24},{24,28},{28,32},{32,36}... | collective-permute-start | bytes 1179656 | tf_op jit(solution)/shard_map/ppermute | solution.py:24
  40.1 7.0 %collective-permute-start.1 = (f32[3,1,256,128]{3,2,1,0:T(8,128)}, f32[3,1,256,128]{3,2,1,0:T(8,128)S(1)}, u32[]{:S(2)}, u32[]{:S(2)}) collective-permute-start(f32[3,1,256,128]{3,2,1,0:T(8,128)} %get-tuple-element.87), channel_id=1, source_target_pairs={{4,0},{8,4},{12,8},{16,12},{20,16},{24,20},{28,24},{32,28},{36,32}... | collective-permute-start | bytes 1179656 | tf_op jit(solution)/shard_map/ppermute | solution.py:25
  47.1 0.9 slice_bitcast_fusion.2
  48.2 0.6 fusion.60
  48.9 0.2 copy.270
  49.1 0.2 copy.269
  49.3 0.3 maximum_bitcast_fusion
  49.6 0.6 pad_clamp_fusion
  50.2 0.3 copy.271
  50.7 0.9 scatter_custom_fusion
  51.6 0.8 reshape.268
  52.4 0.1 reshape.276
  52.8 1.3 scatter_custom_fusion.2
  54.2 0.9 copy.295
  55.1 2.1 and_reduce_fusion
  57.3 18.1 %all-to-all-start.3 = ((bf16[128,2,16]{2,1,0:T(2,128)(2,1)}), bf16[128,2,16]{2,1,0:T(2,128)(2,1)S(1)}, u32[]{:S(2)}, u32[]{:S(2)}) async-start(bf16[128,2,16]{2,1,0:T(2,128)(2,1)} %bitcast.30), calls=%async_computation.3 | async-start | bytes 131072 | tf_op jit(solution)/shard_map/all_to_all | solution.py:157
  75.4 14.9 %all-to-all-done.3 = bf16[128,2,16]{2,1,0:T(2,128)(2,1)S(1)} async-done(((bf16[128,2,16]{2,1,0:T(2,128)(2,1)}), bf16[128,2,16]{2,1,0:T(2,128)(2,1)S(1)}, u32[]{:S(2)}, u32[]{:S(2)}) %all-to-all-start.3) | async-done | bytes 8224 | tf_op jit(solution)/shard_map/all_to_all | solution.py:157
  90.4 7.2 %all-to-all-start = ((bf16[128,2,384]{2,1,0:T(2,128)(2,1)}), bf16[128,2,384]{2,1,0:T(2,128)(2,1)}, u32[]{:S(2)}, u32[]{:S(2)}) async-start(bf16[128,2,384]{2,1,0:T(2,128)(2,1)} %reshape.268), calls=%async_computation | async-start | bytes 393216 | tf_op jit(solution)/shard_map/all_to_all | solution.py:156
  97.6 2.2 fusion.57
  99.8 1.9 copy.264
  101.7 5.5 %collective-permute-start.2 = (f32[3,4,256,1]{2,1,3,0:T(4,128)S(1)}, f32[3,4,256,1]{2,1,3,0:T(4,128)}, u32[]{:S(2)}, u32[]{:S(2)}) collective-permute-start(f32[3,4,256,1]{2,1,3,0:T(4,128)S(1)} %copy.264), channel_id=1, source_target_pairs={{1,0},{2,1},{3,2},{0,3},{5,4},{6,5},{7,6},{4,7},{9,8},{10,9},{11,1... | collective-permute-start | bytes 36872 | tf_op jit(solution)/shard_map/ppermute | solution.py:25
  107.2 2.5 %copy.266 = f32[3,4,256,1]{2,1,3,0:T(4,128)} copy(f32[3,4,256,1]{3,2,1,0:T(8,128)} %get-tuple-element.80) | data formatting | bytes 24576 | tf_op jit(solution)/shard_map/slice | solution.py:22
  109.7 2.4 %collective-permute-start.3 = (f32[3,4,256,1]{2,1,3,0:T(4,128)}, f32[3,4,256,1]{2,1,3,0:T(4,128)}, u32[]{:S(2)}, u32[]{:S(2)}) collective-permute-start(f32[3,4,256,1]{2,1,3,0:T(4,128)} %copy.266), channel_id=1, source_target_pairs={{0,1},{1,2},{2,3},{3,0},{4,5},{5,6},{6,7},{7,4},{8,9},{9,10},{10,1... | collective-permute-start | bytes 36872 | tf_op jit(solution)/shard_map/ppermute | solution.py:24
  112.1 0.2 multiply_reduce_fusion
  112.3 0.7 mul.210
  113.1 0.3 copy.294
  113.3 0.6 reshape.281
  114.0 2.4 %copy.265 = f32[3,4,256,1]{3,2,1,0:T(8,128)} copy(f32[3,4,256,1]{2,1,3,0:T(4,128)} %collective-permute-done.2) | data formatting | bytes 24576 | tf_op jit(solution)/shard_map/ppermute | solution.py:25
  116.4 2.3 %copy.267 = f32[3,4,256,1]{3,2,1,0:T(8,128)} copy(f32[3,4,256,1]{2,1,3,0:T(4,128)} %collective-permute-done.3) | data formatting | bytes 24576 | tf_op jit(solution)/shard_map/ppermute | solution.py:24
  118.7 2.6 %subtract_add_fusion = f32[3,2,256,128]{3,2,1,0:T(8,128)S(1)} fusion(f32[3,2,256,128]{3,2,1,0:T(8,128)S(1)} %copy-done.1, f32[3,2,1,128]{3,2,1,0:T(1,128)S(1)} %get-tuple-element.83, f32[3,2,1,128]{3,2,1,0:T(1,128)S(1)} %get-tuple-element.82, f32[3,1,256,128]{3,2,1,0:T(8,128)} %copy-done.2, f32[3,1,256,128]{3,2,1,0:T(8,128)} %copy-done.3, ...), kind=kLoop, calls=%fused_computation.50 | loop fusion | flops 4915200 | bytes 4749324 | tf_op jit(solution)/shard_map/add | solution.py:67
  121.4 1.4 reshape.269
  122.8 0.3 copy.273
  123.4 0.7 multiply_convert_fusion.1
  124.4 0.8 copy-done.6
  125.3 1.1 add_convert_fusion
  126.4 0.2 multiply_convert_fusion.3
  126.6 0.6 multiply_convert_fusion
  127.2 2.2 fusion.2
  129.8 0.8 copy-done.7
  130.6 1.2 fusion.8
  131.8 1.3 fusion.9
  133.1 1.0 reshape.270
  134.2 1.6 copy.278
  135.7 18.8 %all-to-all-start.1 = ((f32[128,2,16]{2,1,0:T(2,128)}), f32[128,2,16]{2,1,0:T(2,128)S(1)}, u32[]{:S(2)}, u32[]{:S(2)}) async-start(f32[128,2,16]{2,1,0:T(2,128)} %copy.278), calls=%async_computation.1 | async-start | bytes 262144 | tf_op jit(solution)/shard_map/all_to_all | solution.py:169
  154.5 0.2 convolution_bitcast_fusion
  154.8 0.4 all-reduce.6.cloned.1.call-update
  155.2 6.0 %psum.23 = f32[1,128,2]{1,2,0:T(2,128)} all-reduce(f32[1,128,2]{1,2,0:T(2,128)S(1)} %convolution_bitcast_fusion), channel_id=1, replica_groups=mesh['les'=128,'cnn'=4] {'cnn'}, use_global_device_ids=true, to_apply=%region_7.8 | all-reduce | flops 256 | bytes 2048 | tf_op jit(solution)/shard_map/psum | solution.py:191
  161.2 8.9 %all-to-all-done.1 = f32[128,2,16]{2,1,0:T(2,128)S(1)} async-done(((f32[128,2,16]{2,1,0:T(2,128)}), f32[128,2,16]{2,1,0:T(2,128)S(1)}, u32[]{:S(2)}, u32[]{:S(2)}) %all-to-all-start.1) | async-done | bytes 16416 | tf_op jit(solution)/shard_map/all_to_all | solution.py:169
  170.1 0.7 gather_fusion
  171.0 0.1 copy.280
  171.4 1.3 constant_dynamic-slice_fusion
  172.7 0.7 add_select_fusion
  173.4 1.3 scatter-add.16
  174.8 1.0 multiply_add_fusion
  175.8 38.6 %all-reduce.6.cloned.1.call-done = (f32[1,432,128]{2,1,0:T(8,128)}, f32[1,1152,128]{2,1,0:T(8,128)}) async-done(((f32[1,432,128]{2,1,0:T(8,128)}, f32[1,1152,128]{2,1,0:T(8,128)}), (f32[1,432,128]{2,1,0:T(8,128)}, f32[1,1152,128]{2,1,0:T(8,128)})) %all-reduce.6.cloned.1.call-update) | async-done | bytes 811024 | tf_op jit(solution)/shard_map/psum | solution.py:191
  214.3 1.6 copy.377
  216.0 1.9 copy.378
  (91 shorter events, 2.2 us)
Async XLA Ops:
  7.2 116.2 %copy-start = (bf16[1,432,128]{2,1,0:T(8,128)(2,1)S(1)}, bf16[1,432,128]{2,1,0:T(8,128)(2,1)}, u32[]{:S(2)}) copy-start(bf16[1,432,128]{2,1,0:T(8,128)(2,1)} %param.22) | copy-start | bytes 331780
  7.2 39.9 %copy-start.1 = (f32[3,2,256,128]{3,2,1,0:T(8,128)S(1)}, f32[3,2,256,128]{3,2,1,0:T(8,128)}, u32[]{:S(2)}) copy-start(f32[3,2,256,128]{3,2,1,0:T(8,128)} %param.18) | copy-start | bytes 2359300
  7.2 40.8 %slice-start = ((f32[3,2,256,128]{3,2,1,0:T(8,128)}), f32[3,2,16,128]{3,2,1,0:T(8,128)S(1)}, s32[]{:S(2)}) async-start(f32[3,2,256,128]{3,2,1,0:T(8,128)} %param.18), calls=%async_computation.5 | async-start | bytes 98304 | tf_op jit(solution)/shard_map/slice | solution.py:122
  10.4 37.6 %copy-start.10 = (f32[3]{0:T(128)S(1)}, f32[3]{0:T(128)}, u32[]{:S(2)}) copy-start(f32[3]{0:T(128)} %constant.153.clone) | copy-start | bytes 40
  11.2 46.0 %all-to-all-start.2 = ((bf16[128,1,2]{2,1,0:T(2,128)(2,1)}), bf16[128,1,2]{2,1,0:T(2,128)(2,1)S(1)}, u32[]{:S(2)}, u32[]{:S(2)}) async-start(bf16[128,1,2]{2,1,0:T(2,128)(2,1)} %all_to_all.20), calls=%async_computation.2 | async-start | bytes 131072 | tf_op jit(solution)/shard_map/all_to_all | solution.py:158
  36.1 21.1 %collective-permute-start = (f32[3,1,256,128]{3,2,1,0:T(8,128)S(1)}, f32[3,1,256,128]{3,2,1,0:T(8,128)S(1)}, u32[]{:S(2)}, u32[]{:S(2)}) collective-permute-start(f32[3,1,256,128]{3,2,1,0:T(8,128)S(1)} %get-tuple-element.88), channel_id=1, source_target_pairs={{0,4},{4,8},{8,12},{12,16},{16,20},{20,24},{24,28},{28,32},{32,36}... | collective-permute-start | bytes 1179656 | tf_op jit(solution)/shard_map/ppermute | solution.py:24
  40.1 35.3 %collective-permute-start.1 = (f32[3,1,256,128]{3,2,1,0:T(8,128)}, f32[3,1,256,128]{3,2,1,0:T(8,128)S(1)}, u32[]{:S(2)}, u32[]{:S(2)}) collective-permute-start(f32[3,1,256,128]{3,2,1,0:T(8,128)} %get-tuple-element.87), channel_id=1, source_target_pairs={{4,0},{8,4},{12,8},{16,12},{20,16},{24,20},{28,24},{32,28},{36,32}... | collective-permute-start | bytes 1179656 | tf_op jit(solution)/shard_map/ppermute | solution.py:25
  48.0 4.3 %copy-start.11 = (bf16[2,2,128,2]{2,3,1,0:T(2,128)(2,1)S(1)}, bf16[2,2,128,2]{2,3,1,0:T(2,128)(2,1)}, u32[]{:S(2)}) copy-start(bf16[2,2,128,2]{2,3,1,0:T(2,128)(2,1)} %param.19) | copy-start | bytes 6148
  48.0 6.2 %copy-start.5 = (bf16[1,1152,128]{2,1,0:T(8,128)(2,1)S(1)}, bf16[1,1152,128]{2,1,0:T(8,128)(2,1)}, u32[]{:S(2)}) copy-start(bf16[1,1152,128]{2,1,0:T(8,128)(2,1)} %param.23) | copy-start | bytes 884740
  49.0 6.0 %copy-start.14 = (s32[4]{0:T(128)S(1)}, s32[4]{0:T(128)}, u32[]{:S(2)}) copy-start(s32[4]{0:T(128)} %constant.148.clone.1) | copy-start | bytes 52
  57.2 33.2 %copy-start.2 = (f32[3,1,256,128]{3,2,1,0:T(8,128)}, f32[3,1,256,128]{3,2,1,0:T(8,128)S(1)}, u32[]{:S(2)}) copy-start(f32[3,1,256,128]{3,2,1,0:T(8,128)S(1)} %collective-permute-done) | copy-start | bytes 1179652
  57.3 33.1 %all-to-all-start.3 = ((bf16[128,2,16]{2,1,0:T(2,128)(2,1)}), bf16[128,2,16]{2,1,0:T(2,128)(2,1)S(1)}, u32[]{:S(2)}, u32[]{:S(2)}) async-start(bf16[128,2,16]{2,1,0:T(2,128)(2,1)} %bitcast.30), calls=%async_computation.3 | async-start | bytes 131072 | tf_op jit(solution)/shard_map/all_to_all | solution.py:157
  75.4 24.4 %copy-start.3 = (f32[3,1,256,128]{3,2,1,0:T(8,128)}, f32[3,1,256,128]{3,2,1,0:T(8,128)S(1)}, u32[]{:S(2)}) copy-start(f32[3,1,256,128]{3,2,1,0:T(8,128)S(1)} %collective-permute-done.1) | copy-start | bytes 1179652
  90.4 31.0 %all-to-all-start = ((bf16[128,2,384]{2,1,0:T(2,128)(2,1)}), bf16[128,2,384]{2,1,0:T(2,128)(2,1)}, u32[]{:S(2)}, u32[]{:S(2)}) async-start(bf16[128,2,384]{2,1,0:T(2,128)(2,1)} %reshape.268), calls=%async_computation | async-start | bytes 393216 | tf_op jit(solution)/shard_map/all_to_all | solution.py:156
  101.7 12.3 %collective-permute-start.2 = (f32[3,4,256,1]{2,1,3,0:T(4,128)S(1)}, f32[3,4,256,1]{2,1,3,0:T(4,128)}, u32[]{:S(2)}, u32[]{:S(2)}) collective-permute-start(f32[3,4,256,1]{2,1,3,0:T(4,128)S(1)} %copy.264), channel_id=1, source_target_pairs={{1,0},{2,1},{3,2},{0,3},{5,4},{6,5},{7,6},{4,7},{9,8},{10,9},{11,1... | collective-permute-start | bytes 36872 | tf_op jit(solution)/shard_map/ppermute | solution.py:25
  109.7 6.7 %collective-permute-start.3 = (f32[3,4,256,1]{2,1,3,0:T(4,128)}, f32[3,4,256,1]{2,1,3,0:T(4,128)}, u32[]{:S(2)}, u32[]{:S(2)}) collective-permute-start(f32[3,4,256,1]{2,1,3,0:T(4,128)} %copy.266), channel_id=1, source_target_pairs={{0,1},{1,2},{2,3},{3,0},{4,5},{5,6},{6,7},{7,4},{8,9},{9,10},{10,1... | collective-permute-start | bytes 36872 | tf_op jit(solution)/shard_map/ppermute | solution.py:24
  113.9 4.8 %copy-start.4 = (f32[2,256,128]{2,1,0:T(8,128)S(1)}, f32[2,256,128]{2,1,0:T(8,128)}, u32[]{:S(2)}) copy-start(f32[2,256,128]{2,1,0:T(8,128)} %get-tuple-element.84) | copy-start | bytes 786436
  114.0 4.8 %copy-start.13 = (f32[3]{0:T(128)S(1)}, f32[3]{0:T(128)}, u32[]{:S(2)}) copy-start(f32[3]{0:T(128)} %constant.154.clone) | copy-start | bytes 40
  124.3 1.0 copy-start.6
  125.3 1.1 copy-start.9
  125.3 1.2 copy-start.12
  129.7 1.0 copy-start.7
  135.7 34.4 %all-to-all-start.1 = ((f32[128,2,16]{2,1,0:T(2,128)}), f32[128,2,16]{2,1,0:T(2,128)S(1)}, u32[]{:S(2)}, u32[]{:S(2)}) async-start(f32[128,2,16]{2,1,0:T(2,128)} %copy.278), calls=%async_computation.1 | async-start | bytes 262144 | tf_op jit(solution)/shard_map/all_to_all | solution.py:169
  154.5 59.8 %all-reduce.6.cloned.1.call-start = ((), (), s32[]{:S(2)}) async-start(), calls=%async_computation.4 | async-start | bytes 1622016 | tf_op jit(solution)/shard_map/psum | solution.py:191
  171.2 46.7 %copy-start.8 = (f32[2,2,128,2]{2,3,1,0:T(2,128)}, f32[2,2,128,2]{2,3,1,0:T(2,128)S(1)}, u32[]{:S(2)}) copy-start(f32[2,2,128,2]{2,3,1,0:T(2,128)S(1)} %reshape.273) | copy-start | bytes 12292
Sparse Core Ops, SparseCore 0:
  158.9 55.3 all-reduce.5
where the time goes:
time: 226 us; the launch traced here: 225 us
  starting transfers between devices  86 us (38%)
  waiting for transfers between devices  62.9 us (28%)
  local copies, waits for them, and re-layouts  37.7 us (17%)
  between operations  14.7 us (7%)
  other arithmetic  9.96 us (4%)
  matrix products  7.48 us (3%)
  blocking collectives  5.97 us (3%)
    psum x1, waiting for transfers between devices, per_device(): summed = lax.psum((grads[0], grads[1], grads[2]), 'cnn')  38.6 us
    all_to_all x1, starting transfers between devices, wall_models(): lax.all_to_all(send_mask, 'les', split_axis=0, concat_axis=0, tiled=True)  23 us
    all_to_all x1, starting transfers between devices, wall_models(): lax.all_to_all(predicted.reshape(owners_count, capacity, -1), 'les', spli...  18.8 us
    all_to_all x1, starting transfers between devices, wall_models(): lax.all_to_all(send_targets, 'les', split_axis=0, concat_axis=0, tiled=True)  18.1 us
    all_to_all x1, waiting for transfers between devices, wall_models(): lax.all_to_all(send_targets, 'les', split_axis=0, concat_axis=0, tiled=True)  14.9 us
    ppermute x2, starting transfers between devices, extended(): after = lax.ppermute(initial, axis, down)  12.6 us
    all_to_all x1, waiting for transfers between devices, wall_models(): lax.all_to_all(predicted.reshape(owners_count, capacity, -1), 'les', spli...  8.9 us
    all_to_all x1, starting transfers between devices, wall_models(): lax.all_to_all(send_data, 'les', split_axis=0, concat_axis=0, tiled=True)  7.22 us
  transfers between devices with their start and end apart: 9, of which 3 were waited for; matrix products, arithmetic and copies ran while one was open for 15% of the time, Pallas kernels for 0%

commit v1 on v0

v1 whole, which is shorter than its diff:
```python
import functools
import math

import jax
import jax.numpy as jnp
from jax import lax
from jax.experimental import pallas as pl
from jax.experimental.pallas import tpu as pltpu
from jax.sharding import PartitionSpec as P

TX = 4
NPL = 16
CZ = 2
NCNN = 4
C = 128
CIN = 48
CAP = 2
DT_STEP = 0.25
VISCOSITY = 0.05
FORCING = 0.2
GHOST = 8
LANES = 512
PRED = 128
MESH = pl.DeviceIdType.MESH
F32 = jnp.float32
BF16 = jnp.bfloat16


def z_extent(les_size):
    return 16 if les_size == 128 else 2


def dot(a, b):
    return lax.dot_general(a, b, (((1,), (0,)), ((), ())), preferred_element_type=F32)


def dot_nt(a, b):
    return lax.dot_general(a, b, (((1,), (1,)), ((), ())), preferred_element_type=F32)


def dot_tn(a, b):
    return lax.dot_general(a, b, (((0,), (0,)), ((), ())), preferred_element_type=F32)


def iota(shape, dim):
    return lax.broadcasted_iota(jnp.int32, shape, dim)


def log2(n):
    return n.bit_length() - 1


def gate(values):
    logistic = 0.5 * jnp.tanh(0.5 * values) + 0.5
    return values * logistic, logistic * (1.0 + values * (1.0 - logistic))


def kernel(
    own_ref, ord_ref, tgt_ref, wo_ref, vel_hbm, wf_hbm, wm_hbm,
    ws_ref, go_ref, nv_hbm, gf_hbm, gm_hbm,
    walls, v, nv, wf, wm, t_one, m_fwd, m_bwd, wo_t, sel,
    s1, x1, z0, z1, r0, r1, r2, r3, hs, hr, xs, xr,
    h_one, h_one_t, h_two, slope_one, slope_two, g_two, gp_two,
    m_part, m_in, m_send, m_got, m_tot, f_part, f_in, f_send, f_got, f_tot,
    local_sem, q_send, q_recv, zs_send, zs_recv, rz_send, rz_recv, rq_send, rq_recv,
    halo_send, halo_recv, grad_send, grad_recv,
):
    les_size = lax.axis_size("les")
    zn = z_extent(les_size)
    qn = les_size // zn
    rows = CAP * les_size
    _, _, ny, cx = vel_hbm.shape
    tiles = 2 * cx // TX
    both = 2 * cx
    loss_scale = 1.0 / math.sqrt(TX * CZ * tiles * NCNN)

    les, cnn = lax.axis_index("les"), lax.axis_index("cnn")
    z, q = les // qn, les % qn
    right, left = (les + 1) % les_size, (les + les_size - 1) % les_size
    east, west, across = (cnn + 1) % NCNN, (cnn + 3) % NCNN, (cnn + 2) % NCNN
    core = cnn % 2
    other = 1 - core
    twin = cnn + 1 - 2 * core

    def q_peer(step):
        return (q + step) % qn

    def z_peer(step):
        return (z + step) % zn

    far_first = sorted(range(1, zn), key=lambda s: -min(s, zn - s))

    barrier = pltpu.get_barrier_semaphore()
    greeted = 0
    for step in range(1, qn):
        pl.semaphore_signal(barrier, 1, device_id={"les": z * qn + q_peer(step)}, device_id_type=MESH)
        greeted += 1
    for step in range(1, zn):
        pl.semaphore_signal(barrier, 1, device_id={"les": z_peer(step) * qn + q}, device_id_type=MESH)
        greeted += 1
    for peer in (left, right):
        pl.semaphore_signal(barrier, 1, device_id={"les": peer}, device_id_type=MESH)
        greeted += 1
    for step in range(1, NCNN):
        pl.semaphore_signal(barrier, 1, device_id={"cnn": (cnn + step) % NCNN}, device_id_type=MESH)
        greeted += 1

    low_copy = pltpu.make_async_copy(vel_hbm.at[:, :, pl.ds(0, NPL), :], walls.at[0], local_sem.at[0])
    high_copy = pltpu.make_async_copy(vel_hbm.at[:, :, pl.ds(ny - NPL, NPL), :], walls.at[1], local_sem.at[1])
    v_copy = pltpu.make_async_copy(vel_hbm, v.at[:, :, pl.ds(GHOST, ny), :], local_sem.at[2])
    wf_copy = pltpu.make_async_copy(wf_hbm, wf, local_sem.at[3])
    wm_copy = pltpu.make_async_copy(wm_hbm, wm, local_sem.at[4])
    for copy in (low_copy, high_copy, v_copy, wf_copy, wm_copy):
        copy.start()

    own_row = own_ref[...].astype(F32)
    train_row = jnp.where(ord_ref[...] < tiles // 2, 1.0, 0.0)
    eye = iota((tiles, tiles), 0) == iota((tiles, tiles), 1)
    own_col = jnp.sum(jnp.where(eye, own_row, 0.0), axis=1, keepdims=True)
    train_col = jnp.sum(jnp.where(eye, train_row, 0.0), axis=1, keepdims=True)
    lane_tile = iota((tiles, both), 1) >> log2(TX)
    tile_row = iota((tiles, both), 0)
    hit = lane_tile == tile_row
    own_lane = jnp.sum(jnp.where(hit, own_col, 0.0), axis=0, keepdims=True)
    train_lane = jnp.sum(jnp.where(hit, train_col, 0.0), axis=0, keepdims=True)
    before = jnp.logical_and(own_col == own_lane, tile_row < lane_tile)
    rank_lane = jnp.sum(jnp.where(before, 1.0, 0.0), axis=0, keepdims=True).astype(jnp.int32)
    owner = own_lane.astype(jnp.int32)
    slot = (owner & (qn - 1)) * (CAP * zn) + (owner >> log2(qn)) * CAP + rank_lane
    sel[...] = jnp.where(iota((rows, both), 0) == slot, 1.0, 0.0).astype(BF16)

    low_copy.wait()
    high_copy.wait()
    planes = CZ * 3 * NPL
    order = [(zz, c) for zz in range(CZ) for c in range(3)]
    low = jnp.concatenate([walls[0, c, zz] for zz, c in order], axis=0).astype(BF16)
    high = jnp.concatenate([walls[1, c, zz] for zz, c in order], axis=0).astype(BF16)
    fr, fc = iota((planes, planes), 0), iota((planes, planes), 1)
    group = fr >> log2(NPL)
    turned = jnp.logical_and(group == (fc >> log2(NPL)), (fr & (NPL - 1)) + (fc & (NPL - 1)) == NPL - 1)
    sign = jnp.where(jnp.logical_or(group == 1, group == 4), -1.0, 1.0)
    flip = jnp.where(turned, sign, 0.0).astype(BF16)
    cells = jnp.concatenate([low.astype(F32), dot(flip, high)], axis=1)
    cell_x = iota((planes, both), 1) & (TX - 1)
    pieces = [jnp.where(cell_x == xx, cells, 0.0).astype(BF16) for xx in range(TX)]
    goal = [
        jnp.concatenate([tgt_ref[b, zz].astype(F32) for zz in range(CZ)], axis=0) for b in range(2)
    ]
    goal = jnp.concatenate(goal, axis=1)
    goal = jnp.concatenate([goal] * TX, axis=0)
    small_x = iota((16, both), 1) & (TX - 1)
    small_row = iota((16, both), 0)
    pieces.append(jnp.where(small_x == (small_row >> 2), goal, 0.0).astype(BF16))
    pieces.append(jnp.where(small_x == 0, jnp.broadcast_to(train_lane, (16, both)), 0.0).astype(BF16))
    pieces.append(jnp.zeros((LANES - TX * planes - 32, both), BF16))
    packed = dot_nt(sel[...], jnp.concatenate(pieces, axis=0)).astype(BF16)
    s1[...] = packed.reshape(qn, CAP * zn, LANES)

    pl.semaphore_wait(barrier, greeted)

    sends = []
    q_copies = []
    for step in range(1, qn):
        copy = pltpu.make_async_remote_copy(
            s1.at[q_peer(step)], x1.at[q], q_send.at[step], q_recv.at[step],
            device_id={"les": z * qn + q_peer(step)}, device_id_type=MESH,
        )
        copy.start()
        q_copies.append(copy)
    sends += q_copies
    x1[q] = s1[q]

    v_copy.wait()
    for zz in range(CZ):
        hs[zz] = v[:, zz, GHOST : GHOST + ny, :].astype(BF16)
    halo_copies = [
        pltpu.make_async_remote_copy(
            hs.at[1], hr.at[0], halo_send.at[0], halo_recv.at[0], device_id={"les": right}, device_id_type=MESH
        ),
        pltpu.make_async_remote_copy(
            hs.at[0], hr.at[1], halo_send.at[1], halo_recv.at[1], device_id={"les": left}, device_id_type=MESH
        ),
    ]
    for copy in halo_copies:
        copy.start()
    yl = xs.shape[2]
    per_column = ny // yl
    er, ec = iota((16, cx), 0), iota((16, cx), 1)
    first_or_last = jnp.logical_or(
        jnp.logical_and(er == 0, ec == 0), jnp.logical_and(er == 1, ec == cx - 1)
    )
    edges = jnp.where(first_or_last, 1.0, 0.0).astype(BF16)
    xs[...] = jnp.zeros(xs.shape, F32)
    for c in range(3):
        for zz in range(CZ):
            column = dot_nt(edges, hs[zz, c])
            for part in range(per_column):
                j = (c * CZ + zz) * per_column + part
                for side in range(2):
                    xs[side, j : j + 1, :] = column[side : side + 1, part * yl : (part + 1) * yl]
    x_copies = [
        pltpu.make_async_remote_copy(
            xs.at[1], xr.at[0], halo_send.at[2], halo_recv.at[2], device_id={"cnn": east}, device_id_type=MESH
        ),
        pltpu.make_async_remote_copy(
            xs.at[0], xr.at[1], halo_send.at[3], halo_recv.at[3], device_id={"cnn": west}, device_id_type=MESH
        ),
    ]
    for copy in x_copies:
        copy.start()
    sends += halo_copies + x_copies

    pr, pc = iota((rows, rows), 0), iota((rows, rows), 1)
    moved = ((pr >> 1) & (qn - 1)) * (CAP * zn) + (pr >> log2(CAP * qn)) * CAP + (pr & 1)
    to_z = jnp.where(pc == moved, 1.0, 0.0).astype(BF16)
    back = ((pr >> 1) & (zn - 1)) * (CAP * qn) + (pr >> log2(CAP * zn)) * CAP + (pr & 1)
    to_q = jnp.where(pc == back, 1.0, 0.0).astype(BF16)
    for copy in q_copies:
        copy.wait_recv()
    z0[...] = dot(to_z, x1[...].reshape(rows, LANES)).astype(BF16).reshape(zn, CAP * qn, LANES)
    z_copies = []
    for step in far_first:
        copy = pltpu.make_async_remote_copy(
            z0.at[z_peer(step)], z1.at[z], zs_send.at[step], zs_recv.at[step],
            device_id={"les": z_peer(step) * qn + q}, device_id_type=MESH,
        )
        copy.start()
        z_copies.append(copy)
    sends += z_copies
    z1[z] = z0[z]

    wf_copy.wait()
    wm_copy.wait()
    t_one[...] = jnp.zeros(t_one.shape, BF16)
    for xi in range(TX):
        for zi in range(CZ):
            for xo in range(max(0, xi - 1), min(TX, xi + 2)):
                for zo in range(CZ):
                    tap = 3 * (zi - zo + 1) + (xi - xo + 1)
                    at_row, at_lane = (xi * CZ + zi) * CIN, (xo * CZ + zo) * C
                    t_one[at_row : at_row + CIN, at_lane : at_lane + C] = wf[tap * CIN : (tap + 1) * CIN, :]
    wide = CZ * C
    for dx in (-1, 0, 1):
        for zi in range(CZ):
            for zo in range(CZ):
                tap = 3 * (zi - zo + 1) + (dx + 1)
                block = wm[tap * C : (tap + 1) * C, :]
                m_fwd[(dx + 1) * wide + zi * C : (dx + 1) * wide + (zi + 1) * C, zo * C : (zo + 1) * C] = block
                m_bwd[zi * C : (zi + 1) * C, (1 - dx) * wide + zo * C : (1 - dx) * wide + (zo + 1) * C] = block
    out_w = wo_ref[...].astype(F32)
    wr = iota((PRED, C), 0)
    for cell in range(TX * CZ):
        block = jnp.where(wr == 2 * cell, out_w[0:1], jnp.where(wr == 2 * cell + 1, out_w[1:2], 0.0))
        wo_t[:, cell * C : (cell + 1) * C] = block.astype(BF16)

    def near(x):
        return max(0, x - 1), min(TX, x + 2)

    for copy in z_copies:
        copy.wait_recv()

    got = z1[...].reshape(rows, LANES)
    data = got[:, : TX * planes]
    for x in range(TX):
        lanes = slice(x * wide, (x + 1) * wide)
        value, slope = gate(dot(data, t_one[:, lanes]))
        h_one[:, lanes] = value.astype(BF16)
        slope_one[:, lanes] = slope
    for x in range(TX):
        lanes = slice(x * wide, (x + 1) * wide)
        lo, hi = near(x)
        weights = m_fwd[(lo - x + 1) * wide : (hi - x + 1) * wide, :]
        value, slope = gate(dot(h_one[:, lo * wide : hi * wide], weights))
        h_two[:, lanes] = (value + h_one[:, lanes].astype(F32)).astype(BF16)
        slope_two[:, lanes] = slope
    predicted = dot_nt(h_two[...], wo_t[...])
    r0[...] = predicted.astype(BF16).reshape(zn, CAP * qn, PRED)
    rz_copies = []
    for step in far_first:
        copy = pltpu.make_async_remote_copy(
            r0.at[z_peer(step)], r1.at[z], rz_send.at[step], rz_recv.at[step],
            device_id={"les": z_peer(step) * qn + q}, device_id_type=MESH,
        )
        copy.start()
        rz_copies.append(copy)
    sends += rz_copies
    r1[z] = r0[z]

    extra = got[:, TX * planes : TX * planes + PRED].astype(F32)
    goal = jnp.where(iota((rows, PRED), 1) < 16, extra, 0.0)
    error = ((2.0 * loss_scale) * extra[:, 16:17] * (predicted - goal)).astype(BF16)
    for x in range(TX):
        lanes = slice(x * wide, (x + 1) * wide)
        grad = dot(error, wo_t[:, lanes])
        g_two[:, lanes] = grad
        gp_two[:, lanes] = (grad * slope_two[:, lanes]).astype(BF16)
    h_one_t[...] = h_one[...].T
    half_m = m_part.shape[1]

    def put_m(tap, value):
        start = tap * C
        while value.shape[0]:
            part, at = start // half_m, start % half_m
            take = min(value.shape[0], half_m - at)
            m_part[part, at : at + take, :] = value[:take]
            value, start = value[take:], start + take

    for dx in (-1, 0, 1):
        total = None
        for x in range(TX):
            if 0 <= x + dx < TX:
                term = dot(
                    h_one_t[(x + dx) * wide : (x + dx + 1) * wide, :], gp_two[:, x * wide : (x + 1) * wide]
                )
                total = term if total is None else total + term
        put_m(dx + 1, total[:C, C:])
        put_m(3 + dx + 1, total[:C, :C] + total[C:, C:])
        put_m(6 + dx + 1, total[C:, :C])

    def exchange(src, dst, index, peer):
        copy = pltpu.make_async_remote_copy(
            src, dst, grad_send.at[index], grad_recv.at[index], device_id={"cnn": peer}, device_id_type=MESH
        )
        copy.start()
        sends.append(copy)
        return copy

    m_first = exchange(m_part.at[other], m_in, 0, twin)

    data_t = data.T
    g_first = [None] * 9
    for x in range(TX):
        lanes = slice(x * wide, (x + 1) * wide)
        lo, hi = near(x)
        weights = m_bwd[:, (lo - x + 1) * wide : (hi - x + 1) * wide]
        grad = g_two[:, lanes] + dot_nt(gp_two[:, lo * wide : hi * wide], weights)
        gp_one = (grad * slope_one[:, lanes]).astype(BF16)
        lo_row, hi_row = lo * planes, hi * planes
        product = dot(data_t[lo_row:hi_row], gp_one)
        for xi in range(lo, hi):
            for zi in range(CZ):
                for zo in range(CZ):
                    tap = 3 * (zi - zo + 1) + (xi - x + 1)
                    at_row = (xi - lo) * planes + zi * CIN
                    piece = product[at_row : at_row + CIN, zo * C : (zo + 1) * C]
                    g_first[tap] = piece if g_first[tap] is None else g_first[tap] + piece
    half_f = f_part.shape[1]
    for tap in range(9):
        start, value = tap * CIN, g_first[tap]
        while value.shape[0]:
            part, at = start // half_f, start % half_f
            take = min(value.shape[0], half_f - at)
            f_part[part, at : at + take, :] = value[:take]
            value, start = value[take:], start + take
    cross = dot_tn(error, h_two[...])
    g_out = None
    for cell in range(TX * CZ):
        piece = cross[2 * cell : 2 * cell + 2, cell * C : (cell + 1) * C]
        g_out = piece if g_out is None else g_out + piece
    out_at = 9 * CIN - half_f
    f_part[1, out_at:half_f, :] = jnp.zeros((half_f - out_at, C), F32)
    f_part[1, out_at : out_at + 2, :] = g_out
    f_first = exchange(f_part.at[other], f_in, 1, twin)

    m_first.wait_recv()
    m_send[...] = (m_part[core] + m_in[...]).astype(BF16)
    m_second = exchange(m_send, m_got, 2, across)

    for copy in rz_copies:
        copy.wait_recv()
    r2[...] = dot(to_q, r1[...].reshape(rows, PRED)).astype(BF16).reshape(qn, CAP * zn, PRED)
    rq_copies = []
    for step in range(1, qn):
        copy = pltpu.make_async_remote_copy(
            r2.at[q_peer(step)], r3.at[q], rq_send.at[step], rq_recv.at[step],
            device_id={"les": z * qn + q_peer(step)}, device_id_type=MESH,
        )
        copy.start()
        rq_copies.append(copy)
    sends += rq_copies
    r3[q] = r2[q]

    f_first.wait_recv()
    f_send[...] = (f_part[core] + f_in[...]).astype(BF16)
    f_second = exchange(f_send, f_got, 3, across)

    for c in range(3):
        mirror = -1.0 if c == 1 else 1.0
        for zz in range(CZ):
            v[c, zz, GHOST - 1 : GHOST, :] = mirror * v[c, zz, GHOST : GHOST + 1, :]
            v[c, zz, GHOST + ny : GHOST + ny + 1, :] = mirror * v[c, zz, GHOST + ny - 1 : GHOST + ny, :]
    for copy in halo_copies + x_copies:
        copy.wait_recv()
    columns = [xr[side].T for side in range(2)]
    chunk = min(64, yl)
    lane = iota((chunk, cx), 1)
    for zz in range(CZ):
        for start in range(0, ny, chunk):
            here = slice(GHOST + start, GHOST + start + chunk)
            speed = [v[c, zz, here, :] for c in range(3)]
            for c in range(3):
                center = speed[c]
                j = (c * CZ + zz) * per_column + start // yl
                at = start % yl
                x_minus = jnp.where(
                    lane == 0, columns[0][at : at + chunk, j : j + 1], pltpu.roll(center, 1, 1)
                )
                x_plus = jnp.where(
                    lane == cx - 1, columns[1][at : at + chunk, j : j + 1], pltpu.roll(center, cx - 1, 1)
                )
                y_minus = v[c, zz, GHOST + start - 1 : GHOST + start - 1 + chunk, :]
                y_plus = v[c, zz, GHOST + start + 1 : GHOST + start + 1 + chunk, :]
                if zz == 0:
                    z_minus, z_plus = hr[0, c, start : start + chunk, :].astype(F32), v[c, 1, here, :]
                else:
                    z_minus, z_plus = v[c, 0, here, :], hr[1, c, start : start + chunk, :].astype(F32)
                advect = 0.5 * (
                    speed[0] * (x_plus - x_minus)
                    + speed[1] * (y_plus - y_minus)
                    + speed[2] * (z_plus - z_minus)
                )
                laplace = x_plus + x_minus + z_plus + z_minus + y_plus + y_minus - 6.0 * center
                change = VISCOSITY * laplace - advect
                if c == 0:
                    change = change + FORCING
                nv[c, zz, start : start + chunk, :] = center + DT_STEP * change

    m_second.wait_recv()
    m_tot[core] = m_send[...].astype(F32) + m_got[...].astype(F32)
    m_third = exchange(m_tot.at[core], m_tot.at[core], 4, twin)

    f_second.wait_recv()
    f_tot[core] = f_send[...].astype(F32) + f_got[...].astype(F32)
    f_third = exchange(f_tot.at[core], f_tot.at[core], 5, twin)

    for copy in rq_copies:
        copy.wait_recv()
    arrived = dot_tn(r3[...].reshape(rows, PRED), sel[...])
    wide_x = iota((2 * CZ, both), 1) & (TX - 1)
    stress = jnp.zeros((2 * CZ, both), F32)
    for xx in range(TX):
        stress = jnp.where(wide_x == xx, arrived[xx * 2 * CZ : (xx + 1) * 2 * CZ, :], stress)
    for b in range(2):
        row = 0 if b == 0 else ny - 1
        for zz in range(CZ):
            part = stress[zz * 2 : zz * 2 + 2, b * cx : (b + 1) * cx]
            ws_ref[b, zz] = part
            for m in range(2):
                c = 2 * m
                nv[c, zz, row : row + 1, :] = nv[c, zz, row : row + 1, :] - DT_STEP * part[m : m + 1]
    nv_copy = pltpu.make_async_copy(nv, nv_hbm, local_sem.at[5])
    nv_copy.start()

    m_third.wait_recv()
    gm_copy = pltpu.make_async_copy(m_tot, gm_hbm, local_sem.at[6])
    gm_copy.start()
    f_third.wait_recv()
    gf_low = pltpu.make_async_copy(f_tot.at[0], gf_hbm.at[pl.ds(0, half_f), :], local_sem.at[7])
    gf_high = pltpu.make_async_copy(
        f_tot.at[1, pl.ds(0, out_at), :], gf_hbm.at[pl.ds(half_f, out_at), :], local_sem.at[8]
    )
    gf_low.start()
    gf_high.start()
    go_ref[...] = f_tot[1, out_at : out_at + 2, :]
    for copy in sends:
        copy.wait_send()
    for copy in (nv_copy, gm_copy, gf_low, gf_high):
        copy.wait()


def per_device(velocity, target_stress, owner_map, train_order, w_first, w_mid, w_out):
    les_size = lax.axis_size("les")
    zn = z_extent(les_size)
    qn = les_size // zn
    rows = CAP * les_size
    _, _, ny, cx = velocity.shape
    tiles = owner_map.shape[0]
    hidden = TX * CZ * C
    half_m, half_f = 9 * C // 2, 224
    yl = min(128, ny)
    vmem = pltpu.VMEM
    scratch = [
        vmem((2, 3, CZ, NPL, cx), F32),
        vmem((3, CZ, ny + 2 * GHOST, cx), F32),
        vmem((3, CZ, ny, cx), F32),
        vmem((9 * CIN, C), BF16),
        vmem((9 * C, C), BF16),
        vmem((TX * CZ * CIN, hidden), BF16),
        vmem((3 * CZ * C, CZ * C), BF16),
        vmem((CZ * C, 3 * CZ * C), BF16),
        vmem((PRED, hidden), BF16),
        vmem((rows, 2 * cx), BF16),
        vmem((qn, CAP * zn, LANES), BF16),
        vmem((qn, CAP * zn, LANES), BF16),
        vmem((zn, CAP * qn, LANES), BF16),
        vmem((zn, CAP * qn, LANES), BF16),
        vmem((zn, CAP * qn, PRED), BF16),
        vmem((zn, CAP * qn, PRED), BF16),
        vmem((qn, CAP * zn, PRED), BF16),
        vmem((qn, CAP * zn, PRED), BF16),
        vmem((CZ, 3, ny, cx), BF16),
        vmem((CZ, 3, ny, cx), BF16),
        vmem((2, 16, yl), F32),
        vmem((2, 16, yl), F32),
        vmem((rows, hidden), BF16),
        vmem((hidden, rows), BF16),
        vmem((rows, hidden), BF16),
        vmem((rows, hidden), F32),
        vmem((rows, hidden), F32),
        vmem((rows, hidden), F32),
        vmem((rows, hidden), BF16),
        vmem((2, half_m, C), F32),
        vmem((half_m, C), F32),
        vmem((half_m, C), BF16),
        vmem((half_m, C), BF16),
        vmem((2, half_m, C), F32),
        vmem((2, half_f, C), F32),
        vmem((half_f, C), F32),
        vmem((half_f, C), BF16),
        vmem((half_f, C), BF16),
        vmem((2, half_f, C), F32),
        pltpu.SemaphoreType.DMA((9,)),
        pltpu.SemaphoreType.DMA((qn,)),
        pltpu.SemaphoreType.DMA((qn,)),
        pltpu.SemaphoreType.DMA((zn,)),
        pltpu.SemaphoreType.DMA((zn,)),
        pltpu.SemaphoreType.DMA((zn,)),
        pltpu.SemaphoreType.DMA((zn,)),
        pltpu.SemaphoreType.DMA((qn,)),
        pltpu.SemaphoreType.DMA((qn,)),
        pltpu.SemaphoreType.DMA((4,)),
        pltpu.SemaphoreType.DMA((4,)),
        pltpu.SemaphoreType.DMA((6,)),
        pltpu.SemaphoreType.DMA((6,)),
    ]
    in_vmem = pl.BlockSpec(memory_space=pltpu.VMEM)
    anywhere = pl.BlockSpec(memory_space=pl.ANY)
    stress, grad_out, new_velocity, grad_first, grad_mid = pl.pallas_call(
        kernel,
        out_shape=(
            jax.ShapeDtypeStruct((2, CZ, 2, cx), F32),
            jax.ShapeDtypeStruct((2, C), F32),
            jax.ShapeDtypeStruct(velocity.shape, F32),
            jax.ShapeDtypeStruct((9 * CIN, C), F32),
            jax.ShapeDtypeStruct((2, half_m, C), F32),
        ),
        in_specs=[in_vmem] * 4 + [anywhere] * 3,
        out_specs=(in_vmem, in_vmem, anywhere, anywhere, anywhere),
        scratch_shapes=scratch,
        compiler_params=pltpu.CompilerParams(
            collective_id=0, has_side_effects=True, vmem_limit_bytes=60 * 2**20
        ),
    )(
        owner_map.reshape(1, tiles),
        train_order,
        target_stress.transpose(0, 1, 3, 2),
        w_out[0].T,
        velocity,
        w_first[0],
        w_mid[0],
    )
    return (
        new_velocity,
        stress.transpose(0, 1, 3, 2),
        grad_first[None],
        grad_mid.reshape(1, 9 * C, C),
        grad_out.T[None],
    )


def solution(mesh):
    placed = (
        P(None, "les", None, "cnn"),
        P(None, "les", "cnn", None),
        P(("les", "cnn"), None),
        P(("les", "cnn"), None),
        P("les", None, None),
        P("les", None, None),
        P("les", None, None),
    )
    return jax.shard_map(
        per_device,
        mesh=mesh,
        in_specs=placed,
        out_specs=(
            P(None, "les", None, "cnn"),
            P(None, "les", "cnn", None),
            P("les", None, None),
            P("les", None, None),
            P("les", None, None),
        ),
        check_vma=False,
    )
```

time: 226 us -> 60.8 us (0.27)
  starting transfers between devices: 86 us -> 0 us
  waiting for transfers between devices: 62.9 us -> 0 us
  Pallas kernels: 0 us -> 55 us
  local copies, waits for them, and re-layouts: 37.7 us -> 4.81 us
  between operations: 14.7 us -> 0.67 us
  other arithmetic: 9.96 us -> 0 us
  matrix products: 7.48 us -> 0 us
  blocking collectives: 5.97 us -> 0 us
    all_to_all x4 -> x0, starting transfers between devices: 67 us -> none  [the longest x1 23 us: wall_models(): lax.all_to_all(send_mask, 'les', split_axis=0, concat_axis=0, tiled=True)]
    pallas_call x0 -> x1, Pallas kernels: none -> 55 us  [per_device(): pl.pallas_call(kernel, out_shape=(jax.ShapeDtypeStruct((2, CZ, 2, cx), F3...]
    psum x1 -> x0, waiting for transfers between devices: 38.6 us -> none  [per_device(): summed = lax.psum((grads[0], grads[1], grads[2]), 'cnn')]
    all_to_all x4 -> x0, waiting for transfers between devices: 23.8 us -> none  [the longest x1 14.9 us: wall_models(): lax.all_to_all(send_targets, 'les', split_axis=0, concat_axis=0, tiled=True)]
    ppermute x4 -> x0, starting transfers between devices: 18.9 us -> none  [the longest x2 12.6 us: extended(): after = lax.ppermute(initial, axis, down)]
    slice x10 -> x0, local copies, waits for them, and re-layouts: 8.66 us -> none  [the longest x2 4.66 us: extended(): last = lax.slice_in_dim(value, length - width, length, axis=dim)]
    dot_general x8 -> x0, matrix products: 7.48 us -> none  [the longest x1 2.21 us: expert_pass(): jnp.einsum('sztk,sztc->kc', middle, grad_pre_two, preferred_element_type=...]
    psum x1 -> x0, blocking collectives: 5.97 us -> none  [per_device(): summed = lax.psum((grads[0], grads[1], grads[2]), 'cnn')]
  transfers between devices with their start and end apart: 9 -> 0, of which waited for: 3 -> 0; matrix products, arithmetic and copies ran while one was open for 15% -> 0% of each run, Pallas kernels for 0% -> 0%
where the time goes in v1:
time: 60.8 us; the launch traced here: 60.4 us
  Pallas kernels  55 us (90%)
  local copies, waits for them, and re-layouts  4.81 us (8%)
  between operations  0.67 us (1%)
    pallas_call x1, Pallas kernels, per_device(): pl.pallas_call(kernel, out_shape=(jax.ShapeDtypeStruct((2, CZ, 2, cx), F3...  55 us
    unnamed x13, local copies, waits for them, and re-layouts  4.81 us

profile of v1, /device:TPU:1, one launch (start us, length us, event | category | flops | bytes accessed | tf_op | source)
XLA Modules:
  0.0 60.4 jit_solution(15501779622985627721)
XLA Ops:
  0.6 55.0 %shard_map.110 = (f32[2,2,2,128]{3,2,1,0:T(2,128)}, f32[2,128]{1,0:T(2,128)}, f32[3,2,256,128]{3,2,1,0:T(8,128)}, f32[432,128]{1,0:T(8,128)}, f32[2,576,128]{2,1,0:T(8,128)}) custom-call(s32[1,64]{1,0:T(1,128)} %bitcast.20, s32[1,64]{1,0:T(1,128)} %ord_ref.1, bf16[2,2,2,128]{3,2,1,0:T(2,128)(2,1)} %bitcast.18, bf16[2,128]{1,0:T(2,128)(2,1)} %bitcast.21, ...), custom_call_target="tpu_custom_call" | custom-call | tf_op jit(solution)/shard_map/pallas_call | solution.py:538
  55.6 0.0 copy-start.2
  55.6 0.0 copy-start.1
  55.6 0.0 copy-start
  55.6 2.1 %copy.17 = f32[3,2,256,128]{3,2,1,0:T(8,128)} copy(f32[3,2,256,128]{3,2,1,0:T(8,128)} %get-tuple-element.20) | data formatting | bytes 1572864
  57.8 0.0 copy-done.2
  57.8 0.6 copy.18
  58.4 0.0 copy-done.1
  58.4 0.7 %copy.19 = f32[1,432,128]{2,1,0:T(8,128)} copy(f32[1,432,128]{2,1,0:T(8,128)S(1)} %bitcast.15) | data formatting | bytes 442368
  59.1 0.0 copy-done
  59.1 0.0 copy-start.3
  59.1 0.8 %copy.20 = f32[1,1152,128]{2,1,0:T(8,128)} copy(f32[1,1152,128]{2,1,0:T(8,128)S(1)} %bitcast.13) | data formatting | bytes 1179648
  59.9 0.0 copy-done.3
  59.9 0.6 copy.21
Async XLA Ops:
  55.6 2.2 %copy-start.2 = (f32[2,2,2,128]{3,2,1,0:T(2,128)S(1)}, f32[2,2,2,128]{3,2,1,0:T(2,128)}, u32[]{:S(2)}) copy-start(f32[2,2,2,128]{3,2,1,0:T(2,128)} %get-tuple-element.11) | copy-start | bytes 12292
  55.6 2.8 %copy-start.1 = (f32[432,128]{1,0:T(8,128)S(1)}, f32[432,128]{1,0:T(8,128)}, u32[]{:S(2)}) copy-start(f32[432,128]{1,0:T(8,128)} %get-tuple-element.12) | copy-start | bytes 663556
  55.6 3.4 %copy-start = (f32[2,576,128]{2,1,0:T(8,128)S(1)}, f32[2,576,128]{2,1,0:T(8,128)}, u32[]{:S(2)}) copy-start(f32[2,576,128]{2,1,0:T(8,128)} %get-tuple-element.13) | copy-start | bytes 1769476
  59.1 0.8 %copy-start.3 = (f32[2,128]{1,0:T(2,128)S(1)}, f32[2,128]{1,0:T(2,128)}, u32[]{:S(2)}) copy-start(f32[2,128]{1,0:T(2,128)} %get-tuple-element.14) | copy-start | bytes 3076

commit v2 on v1

--- a/solution.py
+++ b/solution.py
@@ -19,7 +19,7 @@
 VISCOSITY = 0.05
 FORCING = 0.2
 GHOST = 8
-LANES = 512
+DATA = TX * CZ * CIN
 PRED = 128
 MESH = pl.DeviceIdType.MESH
 F32 = jnp.float32
@@ -56,13 +56,15 @@
 
 
 def kernel(
-    own_ref, ord_ref, tgt_ref, wo_ref, vel_hbm, wf_hbm, wm_hbm,
-    ws_ref, go_ref, nv_hbm, gf_hbm, gm_hbm,
+    own_hbm, ord_hbm, tgt_hbm, wo_hbm, vel_hbm, wf_hbm, wm_hbm,
+    ws_hbm, go_hbm, nv_hbm, gf_hbm, gm_hbm,
+    own_ref, ord_ref, tgt_ref, wo_ref, ws_ref, go_ref,
     walls, v, nv, wf, wm, t_one, m_fwd, m_bwd, wo_t, sel,
-    s1, x1, z0, z1, r0, r1, r2, r3, hs, hr, xs, xr,
+    s1, x1, z0, z1, s1_more, x1_more, z0_more, z1_more, r0, r1, r2, r3, hs, hr, xs, xr,
     h_one, h_one_t, h_two, slope_one, slope_two, g_two, gp_two,
     m_part, m_in, m_send, m_got, m_tot, f_part, f_in, f_send, f_got, f_tot,
-    local_sem, q_send, q_recv, zs_send, zs_recv, rz_send, rz_recv, rq_send, rq_recv,
+    local_sem, q_send, q_recv, qm_send, qm_recv, zs_send, zs_recv, zm_send, zm_recv,
+    rz_send, rz_recv, rq_send, rq_recv,
     halo_send, halo_recv, grad_send, grad_recv,
 ):
     les_size = lax.axis_size("les")
@@ -89,6 +91,7 @@
         return (z + step) % zn
 
     far_first = sorted(range(1, zn), key=lambda s: -min(s, zn - s))
+    q_order = list(range(1, qn))
 
     barrier = pltpu.get_barrier_semaphore()
     greeted = 0
@@ -110,8 +113,16 @@
     v_copy = pltpu.make_async_copy(vel_hbm, v.at[:, :, pl.ds(GHOST, ny), :], local_sem.at[2])
     wf_copy = pltpu.make_async_copy(wf_hbm, wf, local_sem.at[3])
     wm_copy = pltpu.make_async_copy(wm_hbm, wm, local_sem.at[4])
-    for copy in (low_copy, high_copy, v_copy, wf_copy, wm_copy):
+    small_copies = [
+        pltpu.make_async_copy(src, dst, local_sem.at[9 + i])
+        for i, (src, dst) in enumerate(
+            ((own_hbm, own_ref), (ord_hbm, ord_ref), (tgt_hbm, tgt_ref), (wo_hbm, wo_ref))
+        )
+    ]
+    for copy in small_copies + [low_copy, high_copy, v_copy, wf_copy, wm_copy]:
         copy.start()
+    for copy in small_copies:
+        copy.wait()
 
     own_row = own_ref[...].astype(F32)
     train_row = jnp.where(ord_ref[...] < tiles // 2, 1.0, 0.0)
@@ -150,25 +161,48 @@
     goal = jnp.concatenate([goal] * TX, axis=0)
     small_x = iota((16, both), 1) & (TX - 1)
     small_row = iota((16, both), 0)
-    pieces.append(jnp.where(small_x == (small_row >> 2), goal, 0.0).astype(BF16))
-    pieces.append(jnp.where(small_x == 0, jnp.broadcast_to(train_lane, (16, both)), 0.0).astype(BF16))
-    pieces.append(jnp.zeros((LANES - TX * planes - 32, both), BF16))
+    more = [
+        jnp.where(small_x == (small_row >> 2), goal, 0.0).astype(BF16),
+        jnp.where(small_x == 0, jnp.broadcast_to(train_lane, (16, both)), 0.0).astype(BF16),
+        jnp.zeros((PRED - 32, both), BF16),
+    ]
     packed = dot_nt(sel[...], jnp.concatenate(pieces, axis=0)).astype(BF16)
-    s1[...] = packed.reshape(qn, CAP * zn, LANES)
+    s1[...] = packed.reshape(qn, CAP * zn, DATA)
+    packed = dot_nt(sel[...], jnp.concatenate(more, axis=0)).astype(BF16)
+    s1_more[...] = packed.reshape(qn, CAP * zn, PRED)
 
     pl.semaphore_wait(barrier, greeted)
 
     sends = []
-    q_copies = []
-    for step in range(1, qn):
-        copy = pltpu.make_async_remote_copy(
-            s1.at[q_peer(step)], x1.at[q], q_send.at[step], q_recv.at[step],
-            device_id={"les": z * qn + q_peer(step)}, device_id_type=MESH,
-        )
-        copy.start()
-        q_copies.append(copy)
-    sends += q_copies
-    x1[q] = s1[q]
+
+    def spread_q(src, dst, send_sem, recv_sem):
+        copies = []
+        for step in q_order:
+            copy = pltpu.make_async_remote_copy(
+                src.at[q_peer(step)], dst.at[q], send_sem.at[step], recv_sem.at[step],
+                device_id={"les": z * qn + q_peer(step)}, device_id_type=MESH,
+            )
+            copy.start()
+            copies.append(copy)
+        sends.extend(copies)
+        dst[q] = src[q]
+        return copies
+
+    def spread_z(src, dst, send_sem, recv_sem):
+        copies = []
+        for step in far_first:
+            copy = pltpu.make_async_remote_copy(
+                src.at[z_peer(step)], dst.at[z], send_sem.at[step], recv_sem.at[step],
+                device_id={"les": z_peer(step) * qn + q}, device_id_type=MESH,
+            )
+            copy.start()
+            copies.append(copy)
+        sends.extend(copies)
+        dst[z] = src[z]
+        return copies
+
+    q_copies = spread_q(s1, x1, q_send, q_recv)
+    qm_copies = spread_q(s1_more, x1_more, qm_send, qm_recv)
 
     v_copy.wait()
     for zz in range(CZ):
@@ -181,8 +215,6 @@
             hs.at[0], hr.at[1], halo_send.at[1], halo_recv.at[1], device_id={"les": left}, device_id_type=MESH
         ),
     ]
-    for copy in halo_copies:
-        copy.start()
     yl = xs.shape[2]
     per_column = ny // yl
     er, ec = iota((16, cx), 0), iota((16, cx), 1)
@@ -206,9 +238,6 @@
             xs.at[0], xr.at[1], halo_send.at[3], halo_recv.at[3], device_id={"cnn": west}, device_id_type=MESH
         ),
     ]
-    for copy in x_copies:
-        copy.start()
-    sends += halo_copies + x_copies
 
     pr, pc = iota((rows, rows), 0), iota((rows, rows), 1)
     moved = ((pr >> 1) & (qn - 1)) * (CAP * zn) + (pr >> log2(CAP * qn)) * CAP + (pr & 1)
@@ -217,17 +246,15 @@
     to_q = jnp.where(pc == back, 1.0, 0.0).astype(BF16)
     for copy in q_copies:
         copy.wait_recv()
-    z0[...] = dot(to_z, x1[...].reshape(rows, LANES)).astype(BF16).reshape(zn, CAP * qn, LANES)
-    z_copies = []
-    for step in far_first:
-        copy = pltpu.make_async_remote_copy(
-            z0.at[z_peer(step)], z1.at[z], zs_send.at[step], zs_recv.at[step],
-            device_id={"les": z_peer(step) * qn + q}, device_id_type=MESH,
-        )
+    z0[...] = dot(to_z, x1[...].reshape(rows, DATA)).astype(BF16).reshape(zn, CAP * qn, DATA)
+    z_copies = spread_z(z0, z1, zs_send, zs_recv)
+    for copy in qm_copies:
+        copy.wait_recv()
+    z0_more[...] = dot(to_z, x1_more[...].reshape(rows, PRED)).astype(BF16).reshape(zn, CAP * qn, PRED)
+    zm_copies = spread_z(z0_more, z1_more, zm_send, zm_recv)
+    for copy in halo_copies + x_copies:
         copy.start()
-        z_copies.append(copy)
-    sends += z_copies
-    z1[z] = z0[z]
+    sends.extend(halo_copies + x_copies)
 
     wf_copy.wait()
     wm_copy.wait()
@@ -259,8 +286,7 @@
     for copy in z_copies:
         copy.wait_recv()
 
-    got = z1[...].reshape(rows, LANES)
-    data = got[:, : TX * planes]
+    data = z1[...].reshape(rows, DATA)
     for x in range(TX):
         lanes = slice(x * wide, (x + 1) * wide)
         value, slope = gate(dot(data, t_one[:, lanes]))
@@ -275,18 +301,11 @@
         slope_two[:, lanes] = slope
     predicted = dot_nt(h_two[...], wo_t[...])
     r0[...] = predicted.astype(BF16).reshape(zn, CAP * qn, PRED)
-    rz_copies = []
-    for step in far_first:
-        copy = pltpu.make_async_remote_copy(
-            r0.at[z_peer(step)], r1.at[z], rz_send.at[step], rz_recv.at[step],
-            device_id={"les": z_peer(step) * qn + q}, device_id_type=MESH,
-        )
-        copy.start()
-        rz_copies.append(copy)
-    sends += rz_copies
-    r1[z] = r0[z]
-
-    extra = got[:, TX * planes : TX * planes + PRED].astype(F32)
+    rz_copies = spread_z(r0, r1, rz_send, rz_recv)
+
+    for copy in zm_copies:
+        copy.wait_recv()
+    extra = z1_more[...].reshape(rows, PRED).astype(F32)
     goal = jnp.where(iota((rows, PRED), 1) < 16, extra, 0.0)
     error = ((2.0 * loss_scale) * extra[:, 16:17] * (predicted - goal)).astype(BF16)
     for x in range(TX):
@@ -369,16 +388,7 @@
     for copy in rz_copies:
         copy.wait_recv()
     r2[...] = dot(to_q, r1[...].reshape(rows, PRED)).astype(BF16).reshape(qn, CAP * zn, PRED)
-    rq_copies = []
-    for step in range(1, qn):
-        copy = pltpu.make_async_remote_copy(
-            r2.at[q_peer(step)], r3.at[q], rq_send.at[step], rq_recv.at[step],
-            device_id={"les": z * qn + q_peer(step)}, device_id_type=MESH,
-        )
-        copy.start()
-        rq_copies.append(copy)
-    sends += rq_copies
-    r3[q] = r2[q]
+    rq_copies = spread_q(r2, r3, rq_send, rq_recv)
 
     f_first.wait_recv()
     f_send[...] = (f_part[core] + f_in[...]).astype(BF16)
@@ -425,6 +435,12 @@
                     change = change + FORCING
                 nv[c, zz, start : start + chunk, :] = center + DT_STEP * change
 
+    rim = 8
+    body = pltpu.make_async_copy(
+        nv.at[:, :, pl.ds(rim, ny - 2 * rim), :], nv_hbm.at[:, :, pl.ds(rim, ny - 2 * rim), :], local_sem.at[5]
+    )
+    body.start()
+
     m_second.wait_recv()
     m_tot[core] = m_send[...].astype(F32) + m_got[...].astype(F32)
     m_third = exchange(m_tot.at[core], m_tot.at[core], 4, twin)
@@ -448,8 +464,15 @@
             for m in range(2):
                 c = 2 * m
                 nv[c, zz, row : row + 1, :] = nv[c, zz, row : row + 1, :] - DT_STEP * part[m : m + 1]
-    nv_copy = pltpu.make_async_copy(nv, nv_hbm, local_sem.at[5])
-    nv_copy.start()
+    rims = [
+        pltpu.make_async_copy(
+            nv.at[:, :, pl.ds(at, rim), :], nv_hbm.at[:, :, pl.ds(at, rim), :], local_sem.at[13 + i]
+        )
+        for i, at in enumerate((0, ny - rim))
+    ]
+    rims.append(pltpu.make_async_copy(ws_ref, ws_hbm, local_sem.at[15]))
+    for copy in rims:
+        copy.start()
 
     m_third.wait_recv()
     gm_copy = pltpu.make_async_copy(m_tot, gm_hbm, local_sem.at[6])
@@ -462,10 +485,36 @@
     gf_low.start()
     gf_high.start()
     go_ref[...] = f_tot[1, out_at : out_at + 2, :]
+    go_copy = pltpu.make_async_copy(go_ref, go_hbm, local_sem.at[16])
+    go_copy.start()
     for copy in sends:
         copy.wait_send()
-    for copy in (nv_copy, gm_copy, gf_low, gf_high):
+    for copy in rims + [body, gm_copy, gf_low, gf_high, go_copy]:
         copy.wait()
+
+
+def hand_on(*refs):
+    count = (len(refs) - 2) // 3
+    given, results, held = refs[:count], refs[count : 2 * count], refs[2 * count : 3 * count]
+    into, out = refs[-2:]
+    parts = [(i, k) for i in range(count) for k in range(given[i].shape[0] if given[i].shape[0] == 3 else 1)]
+
+    def pick(ref, k):
+        return ref.at[k] if ref.shape[0] == 3 else ref
+
+    loads = [
+        pltpu.make_async_copy(pick(given[i], k), pick(held[i], k), into.at[n]) for n, (i, k) in enumerate(parts)
+    ]
+    stores = [
+        pltpu.make_async_copy(pick(held[i], k), pick(results[i], k), out.at[n]) for n, (i, k) in enumerate(parts)
+    ]
+    for load in loads:
+        load.start()
+    for load, store in zip(loads, stores):
+        load.wait()
+        store.start()
+    for store in stores:
+        store.wait()
 
 
 def per_device(velocity, target_stress, owner_map, train_order, w_first, w_mid, w_out):
@@ -480,6 +529,12 @@
     yl = min(128, ny)
     vmem = pltpu.VMEM
     scratch = [
+        vmem((1, tiles), jnp.int32),
+        vmem((1, tiles), jnp.int32),
+        vmem((2, CZ, 2, cx), BF16),
+        vmem((2, C), BF16),
+        vmem((2, CZ, 2, cx), F32),
+        vmem((2, C), F32),
         vmem((2, 3, CZ, NPL, cx), F32),
         vmem((3, CZ, ny + 2 * GHOST, cx), F32),
         vmem((3, CZ, ny, cx), F32),
@@ -490,10 +545,14 @@
         vmem((CZ * C, 3 * CZ * C), BF16),
         vmem((PRED, hidden), BF16),
         vmem((rows, 2 * cx), BF16),
-        vmem((qn, CAP * zn, LANES), BF16),
-        vmem((qn, CAP * zn, LANES), BF16),
-        vmem((zn, CAP * qn, LANES), BF16),
-        vmem((zn, CAP * qn, LANES), BF16),
+        vmem((qn, CAP * zn, DATA), BF16),
+        vmem((qn, CAP * zn, DATA), BF16),
+        vmem((zn, CAP * qn, DATA), BF16),
+        vmem((zn, CAP * qn, DATA), BF16),
+        vmem((qn, CAP * zn, PRED), BF16),
+        vmem((qn, CAP * zn, PRED), BF16),
+        vmem((zn, CAP * qn, PRED), BF16),
+        vmem((zn, CAP * qn, PRED), BF16),
         vmem((zn, CAP * qn, PRED), BF16),
         vmem((zn, CAP * qn, PRED), BF16),
         vmem((qn, CAP * zn, PRED), BF16),
@@ -519,9 +578,13 @@
         vmem((half_f, C), BF16),
         vmem((half_f, C), BF16),
         vmem((2, half_f, C), F32),
-        pltpu.SemaphoreType.DMA((9,)),
+        pltpu.SemaphoreType.DMA((17,)),
         pltpu.SemaphoreType.DMA((qn,)),
         pltpu.SemaphoreType.DMA((qn,)),
+        pltpu.SemaphoreType.DMA((qn,)),
+        pltpu.SemaphoreType.DMA((qn,)),
+        pltpu.SemaphoreType.DMA((zn,)),
+        pltpu.SemaphoreType.DMA((zn,)),
         pltpu.SemaphoreType.DMA((zn,)),
         pltpu.SemaphoreType.DMA((zn,)),
         pltpu.SemaphoreType.DMA((zn,)),
@@ -533,19 +596,19 @@
         pltpu.SemaphoreType.DMA((6,)),
         pltpu.SemaphoreType.DMA((6,)),
     ]
-    in_vmem = pl.BlockSpec(memory_space=pltpu.VMEM)
     anywhere = pl.BlockSpec(memory_space=pl.ANY)
-    stress, grad_out, new_velocity, grad_first, grad_mid = pl.pallas_call(
+    shapes = (
+        jax.ShapeDtypeStruct((2, CZ, 2, cx), F32),
+        jax.ShapeDtypeStruct((2, C), F32),
+        jax.ShapeDtypeStruct(velocity.shape, F32),
+        jax.ShapeDtypeStruct((9 * CIN, C), F32),
+        jax.ShapeDtypeStruct((2, half_m, C), F32),
+    )
+    results = pl.pallas_call(
         kernel,
-        out_shape=(
-            jax.ShapeDtypeStruct((2, CZ, 2, cx), F32),
-            jax.ShapeDtypeStruct((2, C), F32),
-            jax.ShapeDtypeStruct(velocity.shape, F32),
-            jax.ShapeDtypeStruct((9 * CIN, C), F32),
-            jax.ShapeDtypeStruct((2, half_m, C), F32),
-        ),
-        in_specs=[in_vmem] * 4 + [anywhere] * 3,
-        out_specs=(in_vmem, in_vmem, anywhere, anywhere, anywhere),
+        out_shape=shapes,
+        in_specs=[anywhere] * 7,
+        out_specs=(anywhere,) * 5,
         scratch_shapes=scratch,
         compiler_params=pltpu.CompilerParams(
             collective_id=0, has_side_effects=True, vmem_limit_bytes=60 * 2**20
@@ -559,6 +622,15 @@
         w_first[0],
         w_mid[0],
     )
+    stress, grad_out, new_velocity, grad_first, grad_mid = pl.pallas_call(
+        hand_on,
+        out_shape=shapes,
+        in_specs=[anywhere] * 5,
+        out_specs=(anywhere,) * 5,
+        scratch_shapes=[pltpu.VMEM(s.shape, s.dtype) for s in shapes]
+        + [pltpu.SemaphoreType.DMA((7,)), pltpu.SemaphoreType.DMA((7,))],
+        compiler_params=pltpu.CompilerParams(vmem_limit_bytes=60 * 2**20),
+    )(*results)
     return (
         new_velocity,
         stress.transpose(0, 1, 3, 2),

time: 60.8 us -> 54.9 us (0.903)
  local copies, waits for them, and re-layouts: 4.81 us -> 0 us
  Pallas kernels: 55 us -> 54.1 us
    unnamed x13 -> x0, local copies, waits for them, and re-layouts: 4.81 us -> none
    pallas_call x1 -> x2, Pallas kernels: 55 us -> 54.1 us  [the longest x1 51.8 us: per_device(): pl.pallas_call(kernel, out_shape=shapes, in_specs=[anywhere] * 7, out_spe...]
where the time goes in v2:
time: 54.9 us; the launch traced here: 54.7 us
  Pallas kernels  54.1 us (99%)
  between operations  0.64 us (1%)
    pallas_call x1, Pallas kernels, per_device(): pl.pallas_call(kernel, out_shape=shapes, in_specs=[anywhere] * 7, out_spe...  51.8 us
    pallas_call x1, Pallas kernels, per_device(): pl.pallas_call(hand_on, out_shape=shapes, in_specs=[anywhere] * 5, out_sp...  2.32 us

profile of v2, /device:TPU:1, one launch (start us, length us, event | category | flops | bytes accessed | tf_op | source)
XLA Modules:
  0.0 54.7 jit_solution(13400060263864826294)
XLA Ops:
  0.6 51.8 %shard_map.110 = (f32[2,2,2,128]{3,2,1,0:T(2,128)}, f32[2,128]{1,0:T(2,128)}, f32[3,2,256,128]{3,2,1,0:T(8,128)}, f32[432,128]{1,0:T(8,128)}, f32[2,576,128]{2,1,0:T(8,128)}) custom-call(s32[1,64]{1,0:T(1,128)} %bitcast.16, s32[1,64]{1,0:T(1,128)} %ord_hbm.1, bf16[2,2,2,128]{3,2,1,0:T(2,128)(2,1)} %bitcast.15, bf16[2,128]{1,0:T(2,128)(2,1)} %bitcast.17, ...), custom_call_target="tpu_custom_call" | custom-call | tf_op jit(solution)/shard_map/pallas_call | solution.py:607
  52.4 2.3 %shard_map.111 = (f32[2,2,2,128]{3,2,1,0:T(2,128)}, f32[2,128]{1,0:T(2,128)}, f32[3,2,256,128]{3,2,1,0:T(8,128)}, f32[432,128]{1,0:T(8,128)}, f32[2,576,128]{2,1,0:T(8,128)}) custom-call(f32[2,2,2,128]{3,2,1,0:T(2,128)} %get-tuple-element.15.refs_0_, f32[2,128]{1,0:T(2,128)} %get-tuple-element.16.refs_1_, f32[3,2,256,128]{3,2,1,0:T(8,128)} %get-tuple-element.17.refs_2_, ...), custom_call_target="tpu_custom_call" | custom-call | tf_op jit(solution)/shard_map/pallas_call | solution.py:625

commit v3 on v2

--- a/solution.py
+++ b/solution.py
@@ -59,12 +59,12 @@
     own_hbm, ord_hbm, tgt_hbm, wo_hbm, vel_hbm, wf_hbm, wm_hbm,
     ws_hbm, go_hbm, nv_hbm, gf_hbm, gm_hbm,
     own_ref, ord_ref, tgt_ref, wo_ref, ws_ref, go_ref,
-    walls, v, nv, wf, wm, t_one, m_fwd, m_bwd, wo_t, sel,
-    s1, x1, z0, z1, s1_more, x1_more, z0_more, z1_more, r0, r1, r2, r3, hs, hr, xs, xr,
+    walls, v, nv, wf, wm, t_one, m_fwd, m_bwd, wo_t, sel, from_owner,
+    s1, x1, z0, z1, s1_more, x1_more, z0_more, z1_more, r0, r3, hs, hr, xs, xr,
     h_one, h_one_t, h_two, slope_one, slope_two, g_two, gp_two,
     m_part, m_in, m_send, m_got, m_tot, f_part, f_in, f_send, f_got, f_tot,
     local_sem, q_send, q_recv, qm_send, qm_recv, zs_send, zs_recv, zm_send, zm_recv,
-    rz_send, rz_recv, rq_send, rq_recv,
+    r_send, r_recv,
     halo_send, halo_recv, grad_send, grad_recv,
 ):
     les_size = lax.axis_size("les")
@@ -91,6 +91,11 @@
         return (z + step) % zn
 
     far_first = sorted(range(1, zn), key=lambda s: -min(s, zn - s))
+    turn = zn // 4
+
+    def place(step):
+        return (turn - step) % zn
+
     q_order = list(range(1, qn))
 
     barrier = pltpu.get_barrier_semaphore()
@@ -139,6 +144,10 @@
     owner = own_lane.astype(jnp.int32)
     slot = (owner & (qn - 1)) * (CAP * zn) + (owner >> log2(qn)) * CAP + rank_lane
     sel[...] = jnp.where(iota((rows, both), 0) == slot, 1.0, 0.0).astype(BF16)
+    owner_row = iota((les_size, both), 0)
+    for k in range(CAP):
+        mine = jnp.logical_and(owner_row == owner, rank_lane == k)
+        from_owner[k] = jnp.where(mine, 1.0, 0.0).astype(BF16)
 
     low_copy.wait()
     high_copy.wait()
@@ -192,14 +201,14 @@
         copies = []
         for step in far_first:
             copy = pltpu.make_async_remote_copy(
-                src.at[z_peer(step)], dst.at[z], send_sem.at[step], recv_sem.at[step],
+                src.at[z_peer(step)], dst.at[place(step)], send_sem.at[step], recv_sem.at[step],
                 device_id={"les": z_peer(step) * qn + q}, device_id_type=MESH,
             )
             copy.start()
             copies.append(copy)
         sends.extend(copies)
-        dst[z] = src[z]
-        return copies
+        dst[place(0)] = src[z]
+        return dict(zip(far_first, copies))
 
     q_copies = spread_q(s1, x1, q_send, q_recv)
     qm_copies = spread_q(s1_more, x1_more, qm_send, qm_recv)
@@ -242,8 +251,6 @@
     pr, pc = iota((rows, rows), 0), iota((rows, rows), 1)
     moved = ((pr >> 1) & (qn - 1)) * (CAP * zn) + (pr >> log2(CAP * qn)) * CAP + (pr & 1)
     to_z = jnp.where(pc == moved, 1.0, 0.0).astype(BF16)
-    back = ((pr >> 1) & (zn - 1)) * (CAP * qn) + (pr >> log2(CAP * zn)) * CAP + (pr & 1)
-    to_q = jnp.where(pc == back, 1.0, 0.0).astype(BF16)
     for copy in q_copies:
         copy.wait_recv()
     z0[...] = dot(to_z, x1[...].reshape(rows, DATA)).astype(BF16).reshape(zn, CAP * qn, DATA)
@@ -276,38 +283,75 @@
                 m_bwd[zi * C : (zi + 1) * C, (1 - dx) * wide + zo * C : (1 - dx) * wide + (zo + 1) * C] = block
     out_w = wo_ref[...].astype(F32)
     wr = iota((PRED, C), 0)
+    w16 = jnp.where(wr < CAP * 16, wr & 15, PRED)
     for cell in range(TX * CZ):
-        block = jnp.where(wr == 2 * cell, out_w[0:1], jnp.where(wr == 2 * cell + 1, out_w[1:2], 0.0))
+        block = jnp.where(w16 == 2 * cell, out_w[0:1], jnp.where(w16 == 2 * cell + 1, out_w[1:2], 0.0))
         wo_t[:, cell * C : (cell + 1) * C] = block.astype(BF16)
 
     def near(x):
         return max(0, x - 1), min(TX, x + 2)
 
-    for copy in z_copies:
+    half = rows // 2
+    fold = jnp.where(iota((half // 2, half), 0) == (iota((half // 2, half), 1) >> 1), 1.0, 0.0).astype(BF16)
+    own_lanes = (iota((half, PRED), 1) >> 4) == (iota((half, PRED), 0) & 1)
+    predicted = []
+
+    def forward(top):
+        here = slice(top, top + half)
+        data = z1[top // (CAP * qn) : (top + half) // (CAP * qn)].reshape(half, DATA)
+        for x in range(TX):
+            lanes = slice(x * wide, (x + 1) * wide)
+            value, slope = gate(dot(data, t_one[:, lanes]))
+            h_one[here, lanes] = value.astype(BF16)
+            slope_one[here, lanes] = slope
+        for x in range(TX):
+            lanes = slice(x * wide, (x + 1) * wide)
+            lo, hi = near(x)
+            weights = m_fwd[(lo - x + 1) * wide : (hi - x + 1) * wide, :]
+            value, slope = gate(dot(h_one[here, lo * wide : hi * wide], weights))
+            h_two[here, lanes] = (value + h_one[here, lanes].astype(F32)).astype(BF16)
+            slope_two[here, lanes] = slope
+        result = dot_nt(h_two[here, :], wo_t[...])
+        predicted.append(result)
+        folded = dot(fold, jnp.where(own_lanes, result, 0.0).astype(BF16))
+        r0[top // 2 : (top + half) // 2] = folded.reshape(half // 2, 1, PRED)
+
+    def send_row(row, peer):
+        pltpu.make_async_remote_copy(
+            r0.at[row], r3.at[les], r_send, r_recv, device_id={"les": peer}, device_id_type=MESH
+        ).start()
+
+    def send_places(first, last):
+        def body(p, carry):
+            peer_z = (z + p + zn - turn) % zn
+            for k in range(qn):
+                send_row(p * qn + k, peer_z * qn + k)
+            return carry
+
+        lax.fori_loop(first, last, body, 0)
+
+    for step in far_first:
+        if place(step) < zn // 2:
+            z_copies[step].wait_recv()
+    forward(0)
+    for step in range(1, qn):
+        send_row(turn * qn + q_peer(step), z * qn + q_peer(step))
+    r3[les] = r0[turn * qn + q]
+    send_places(0, turn)
+    send_places(turn + 1, zn // 2)
+    for step in far_first:
+        if place(step) >= zn // 2:
+            z_copies[step].wait_recv()
+    forward(half)
+    send_places(zn // 2, zn)
+
+    for copy in zm_copies.values():
         copy.wait_recv()
-
     data = z1[...].reshape(rows, DATA)
-    for x in range(TX):
-        lanes = slice(x * wide, (x + 1) * wide)
-        value, slope = gate(dot(data, t_one[:, lanes]))
-        h_one[:, lanes] = value.astype(BF16)
-        slope_one[:, lanes] = slope
-    for x in range(TX):
-        lanes = slice(x * wide, (x + 1) * wide)
-        lo, hi = near(x)
-        weights = m_fwd[(lo - x + 1) * wide : (hi - x + 1) * wide, :]
-        value, slope = gate(dot(h_one[:, lo * wide : hi * wide], weights))
-        h_two[:, lanes] = (value + h_one[:, lanes].astype(F32)).astype(BF16)
-        slope_two[:, lanes] = slope
-    predicted = dot_nt(h_two[...], wo_t[...])
-    r0[...] = predicted.astype(BF16).reshape(zn, CAP * qn, PRED)
-    rz_copies = spread_z(r0, r1, rz_send, rz_recv)
-
-    for copy in zm_copies:
-        copy.wait_recv()
+    predicted = jnp.concatenate(predicted, axis=0)
     extra = z1_more[...].reshape(rows, PRED).astype(F32)
-    goal = jnp.where(iota((rows, PRED), 1) < 16, extra, 0.0)
-    error = ((2.0 * loss_scale) * extra[:, 16:17] * (predicted - goal)).astype(BF16)
+    miss = jnp.where(iota((rows, PRED), 1) < 16, predicted - extra, 0.0)
+    error = ((2.0 * loss_scale) * extra[:, 16:17] * miss).astype(BF16)
     for x in range(TX):
         lanes = slice(x * wide, (x + 1) * wide)
         grad = dot(error, wo_t[:, lanes])
@@ -384,11 +428,6 @@
     m_first.wait_recv()
     m_send[...] = (m_part[core] + m_in[...]).astype(BF16)
     m_second = exchange(m_send, m_got, 2, across)
-
-    for copy in rz_copies:
-        copy.wait_recv()
-    r2[...] = dot(to_q, r1[...].reshape(rows, PRED)).astype(BF16).reshape(qn, CAP * zn, PRED)
-    rq_copies = spread_q(r2, r3, rq_send, rq_recv)
 
     f_first.wait_recv()
     f_send[...] = (f_part[core] + f_in[...]).astype(BF16)
@@ -449,9 +488,10 @@
     f_tot[core] = f_send[...].astype(F32) + f_got[...].astype(F32)
     f_third = exchange(f_tot.at[core], f_tot.at[core], 5, twin)
 
-    for copy in rq_copies:
-        copy.wait_recv()
-    arrived = dot_tn(r3[...].reshape(rows, PRED), sel[...])
+    everyone = pl.ds(0, les_size - 1)
+    pltpu.make_async_copy(r0.at[everyone], r3.at[everyone], r_recv).wait()
+    back = r3[...].reshape(les_size, PRED).astype(BF16)
+    arrived = dot_tn(back, from_owner[0])[:16] + dot_tn(back, from_owner[1])[16:32]
     wide_x = iota((2 * CZ, both), 1) & (TX - 1)
     stress = jnp.zeros((2 * CZ, both), F32)
     for xx in range(TX):
@@ -489,6 +529,7 @@
     go_copy.start()
     for copy in sends:
         copy.wait_send()
+    pltpu.make_async_copy(r0.at[everyone], r3.at[everyone], r_send).wait()
     for copy in rims + [body, gm_copy, gf_low, gf_high, go_copy]:
         copy.wait()
 
@@ -545,6 +586,7 @@
         vmem((CZ * C, 3 * CZ * C), BF16),
         vmem((PRED, hidden), BF16),
         vmem((rows, 2 * cx), BF16),
+        vmem((CAP, les_size, 2 * cx), BF16),
         vmem((qn, CAP * zn, DATA), BF16),
         vmem((qn, CAP * zn, DATA), BF16),
         vmem((zn, CAP * qn, DATA), BF16),
@@ -553,10 +595,8 @@
         vmem((qn, CAP * zn, PRED), BF16),
         vmem((zn, CAP * qn, PRED), BF16),
         vmem((zn, CAP * qn, PRED), BF16),
-        vmem((zn, CAP * qn, PRED), BF16),
-        vmem((zn, CAP * qn, PRED), BF16),
-        vmem((qn, CAP * zn, PRED), BF16),
-        vmem((qn, CAP * zn, PRED), BF16),
+        vmem((les_size, 1, PRED), F32),
+        vmem((les_size, 1, PRED), F32),
         vmem((CZ, 3, ny, cx), BF16),
         vmem((CZ, 3, ny, cx), BF16),
         vmem((2, 16, yl), F32),
@@ -587,10 +627,8 @@
         pltpu.SemaphoreType.DMA((zn,)),
         pltpu.SemaphoreType.DMA((zn,)),
         pltpu.SemaphoreType.DMA((zn,)),
-        pltpu.SemaphoreType.DMA((zn,)),
-        pltpu.SemaphoreType.DMA((zn,)),
-        pltpu.SemaphoreType.DMA((qn,)),
-        pltpu.SemaphoreType.DMA((qn,)),
+        pltpu.SemaphoreType.DMA(()),
+        pltpu.SemaphoreType.DMA(()),
         pltpu.SemaphoreType.DMA((4,)),
         pltpu.SemaphoreType.DMA((4,)),
         pltpu.SemaphoreType.DMA((6,)),

time: 54.9 us -> 52.8 us (0.962)
  Pallas kernels: 54.1 us -> 52 us
    pallas_call x1, Pallas kernels: 51.8 us -> 49.7 us  [per_device(): pl.pallas_call(kernel, out_shape=shapes, in_specs=[anywhere] * 7, out_spe...]
where the time goes in v3:
time: 52.8 us; the launch traced here: 52.7 us
  Pallas kernels  52 us (98%)
  between operations  0.64 us (1%)
    pallas_call x1, Pallas kernels, per_device(): pl.pallas_call(kernel, out_shape=shapes, in_specs=[anywhere] * 7, out_spe...  49.7 us
    pallas_call x1, Pallas kernels, per_device(): pl.pallas_call(hand_on, out_shape=shapes, in_specs=[anywhere] * 5, out_sp...  2.32 us

profile of v3, /device:TPU:1, one launch (start us, length us, event | category | flops | bytes accessed | tf_op | source)
XLA Modules:
  0.0 52.7 jit_solution(12602043800640542013)
XLA Ops:
  0.6 49.7 %shard_map.110 = (f32[2,2,2,128]{3,2,1,0:T(2,128)}, f32[2,128]{1,0:T(2,128)}, f32[3,2,256,128]{3,2,1,0:T(8,128)}, f32[432,128]{1,0:T(8,128)}, f32[2,576,128]{2,1,0:T(8,128)}) custom-call(s32[1,64]{1,0:T(1,128)} %bitcast.16, s32[1,64]{1,0:T(1,128)} %ord_hbm.1, bf16[2,2,2,128]{3,2,1,0:T(2,128)(2,1)} %bitcast.15, bf16[2,128]{1,0:T(2,128)(2,1)} %bitcast.17, ...), custom_call_target="tpu_custom_call" | custom-call | tf_op jit(solution)/shard_map/pallas_call | solution.py:645
  50.4 2.3 %shard_map.111 = (f32[2,2,2,128]{3,2,1,0:T(2,128)}, f32[2,128]{1,0:T(2,128)}, f32[3,2,256,128]{3,2,1,0:T(8,128)}, f32[432,128]{1,0:T(8,128)}, f32[2,576,128]{2,1,0:T(8,128)}) custom-call(f32[2,2,2,128]{3,2,1,0:T(2,128)} %get-tuple-element.15.refs_0_, f32[2,128]{1,0:T(2,128)} %get-tuple-element.16.refs_1_, f32[3,2,256,128]{3,2,1,0:T(8,128)} %get-tuple-element.17.refs_2_, ...), custom_call_target="tpu_custom_call" | custom-call | tf_op jit(solution)/shard_map/pallas_call | solution.py:663

commit v4 on v3

--- a/solution.py
+++ b/solution.py
@@ -21,6 +21,7 @@
 GHOST = 8
 DATA = TX * CZ * CIN
 PRED = 128
+MORE = 32
 MESH = pl.DeviceIdType.MESH
 F32 = jnp.float32
 BF16 = jnp.bfloat16
@@ -100,11 +101,11 @@
 
     barrier = pltpu.get_barrier_semaphore()
     greeted = 0
+    for step in far_first:
+        pl.semaphore_signal(barrier, 1, device_id={"les": z_peer(step) * qn + q}, device_id_type=MESH)
+        greeted += 1
     for step in range(1, qn):
         pl.semaphore_signal(barrier, 1, device_id={"les": z * qn + q_peer(step)}, device_id_type=MESH)
-        greeted += 1
-    for step in range(1, zn):
-        pl.semaphore_signal(barrier, 1, device_id={"les": z_peer(step) * qn + q}, device_id_type=MESH)
         greeted += 1
     for peer in (left, right):
         pl.semaphore_signal(barrier, 1, device_id={"les": peer}, device_id_type=MESH)
@@ -173,12 +174,11 @@
     more = [
         jnp.where(small_x == (small_row >> 2), goal, 0.0).astype(BF16),
         jnp.where(small_x == 0, jnp.broadcast_to(train_lane, (16, both)), 0.0).astype(BF16),
-        jnp.zeros((PRED - 32, both), BF16),
     ]
     packed = dot_nt(sel[...], jnp.concatenate(pieces, axis=0)).astype(BF16)
     s1[...] = packed.reshape(qn, CAP * zn, DATA)
     packed = dot_nt(sel[...], jnp.concatenate(more, axis=0)).astype(BF16)
-    s1_more[...] = packed.reshape(qn, CAP * zn, PRED)
+    s1_more[...] = packed.reshape(qn, CAP * zn, MORE)
 
     pl.semaphore_wait(barrier, greeted)
 
@@ -257,7 +257,7 @@
     z_copies = spread_z(z0, z1, zs_send, zs_recv)
     for copy in qm_copies:
         copy.wait_recv()
-    z0_more[...] = dot(to_z, x1_more[...].reshape(rows, PRED)).astype(BF16).reshape(zn, CAP * qn, PRED)
+    z0_more[...] = dot(to_z, x1_more[...].reshape(rows, MORE)).astype(BF16).reshape(zn, CAP * qn, MORE)
     zm_copies = spread_z(z0_more, z1_more, zm_send, zm_recv)
     for copy in halo_copies + x_copies:
         copy.start()
@@ -334,41 +334,41 @@
         if place(step) < zn // 2:
             z_copies[step].wait_recv()
     forward(0)
-    for step in range(1, qn):
-        send_row(turn * qn + q_peer(step), z * qn + q_peer(step))
-    r3[les] = r0[turn * qn + q]
-    send_places(0, turn)
-    send_places(turn + 1, zn // 2)
+    h_one_t[:, :half] = h_one[:half, :].T
     for step in far_first:
         if place(step) >= zn // 2:
             z_copies[step].wait_recv()
     forward(half)
-    send_places(zn // 2, zn)
+    send_places(zn // 2 + turn, zn)
+    send_places(zn // 2, zn // 2 + turn)
 
     for copy in zm_copies.values():
         copy.wait_recv()
     data = z1[...].reshape(rows, DATA)
     predicted = jnp.concatenate(predicted, axis=0)
-    extra = z1_more[...].reshape(rows, PRED).astype(F32)
-    miss = jnp.where(iota((rows, PRED), 1) < 16, predicted - extra, 0.0)
+    extra = z1_more[...].reshape(rows, MORE).astype(F32)
+    miss = predicted[:, :16] - extra[:, :16]
     error = ((2.0 * loss_scale) * extra[:, 16:17] * miss).astype(BF16)
     for x in range(TX):
         lanes = slice(x * wide, (x + 1) * wide)
-        grad = dot(error, wo_t[:, lanes])
+        grad = dot(error, wo_t[:16, lanes])
         g_two[:, lanes] = grad
         gp_two[:, lanes] = (grad * slope_two[:, lanes]).astype(BF16)
-    h_one_t[...] = h_one[...].T
-    half_m = m_part.shape[1]
-
-    def put_m(tap, value):
-        start = tap * C
-        while value.shape[0]:
-            part, at = start // half_m, start % half_m
-            take = min(value.shape[0], half_m - at)
-            m_part[part, at : at + take, :] = value[:take]
-            value, start = value[take:], start + take
-
-    for dx in (-1, 0, 1):
+    h_one_t[:, half:] = h_one[half:, :].T
+
+    def exchange(src, dst, index, peer):
+        copy = pltpu.make_async_remote_copy(
+            src, dst, grad_send.at[index], grad_recv.at[index], device_id={"cnn": peer}, device_id_type=MESH
+        )
+        copy.start()
+        sends.append(copy)
+        return copy
+
+    share = m_in.shape[1]
+    own_part = pl.ds(pl.multiple_of(core * share, share), share)
+    twin_part = pl.ds(pl.multiple_of(other * share, share), share)
+    m_first = []
+    for d, dx in enumerate((-1, 0, 1)):
         total = None
         for x in range(TX):
             if 0 <= x + dx < TX:
@@ -376,19 +376,27 @@
                     h_one_t[(x + dx) * wide : (x + dx + 1) * wide, :], gp_two[:, x * wide : (x + 1) * wide]
                 )
                 total = term if total is None else total + term
-        put_m(dx + 1, total[:C, C:])
-        put_m(3 + dx + 1, total[:C, :C] + total[C:, C:])
-        put_m(6 + dx + 1, total[C:, :C])
-
-    def exchange(src, dst, index, peer):
-        copy = pltpu.make_async_remote_copy(
-            src, dst, grad_send.at[index], grad_recv.at[index], device_id={"cnn": peer}, device_id_type=MESH
-        )
-        copy.start()
-        sends.append(copy)
-        return copy
-
-    m_first = exchange(m_part.at[other], m_in, 0, twin)
+        m_part[d, :C, :] = total[:C, C:]
+        m_part[d, C : 2 * C, :] = total[:C, :C] + total[C:, C:]
+        m_part[d, 2 * C :, :] = total[C:, :C]
+        m_first.append(exchange(m_part.at[d, twin_part], m_in.at[d], d, twin))
+
+    def m_across(d):
+        m_first[d].wait_recv()
+        m_send[d] = (m_part[d, own_part, :] + m_in[d]).astype(BF16)
+        return exchange(m_send.at[d], m_got.at[d], 3 + d, across)
+
+    def m_back(d):
+        m_second[d].wait_recv()
+        m_tot[d, own_part, :] = m_send[d].astype(F32) + m_got[d].astype(F32)
+        return exchange(m_tot.at[d, own_part], m_tot.at[d, own_part], 6 + d, twin)
+
+    send_places(0, turn)
+    send_places(turn + 1, zn // 2)
+    for step in range(1, qn):
+        send_row(turn * qn + q_peer(step), z * qn + q_peer(step))
+    r3[les] = r0[turn * qn + q]
+    m_second = [m_across(0), m_across(1)]
 
     data_t = data.T
     g_first = [None] * 9
@@ -397,6 +405,8 @@
         lo, hi = near(x)
         weights = m_bwd[:, (lo - x + 1) * wide : (hi - x + 1) * wide]
         grad = g_two[:, lanes] + dot_nt(gp_two[:, lo * wide : hi * wide], weights)
+        if x == 1:
+            m_second.append(m_across(2))
         gp_one = (grad * slope_one[:, lanes]).astype(BF16)
         lo_row, hi_row = lo * planes, hi * planes
         product = dot(data_t[lo_row:hi_row], gp_one)
@@ -423,15 +433,16 @@
     out_at = 9 * CIN - half_f
     f_part[1, out_at:half_f, :] = jnp.zeros((half_f - out_at, C), F32)
     f_part[1, out_at : out_at + 2, :] = g_out
-    f_first = exchange(f_part.at[other], f_in, 1, twin)
-
-    m_first.wait_recv()
-    m_send[...] = (m_part[core] + m_in[...]).astype(BF16)
-    m_second = exchange(m_send, m_got, 2, across)
+    f_first = exchange(f_part.at[other], f_in, 9, twin)
+
+    m_third = [m_back(0)]
 
     f_first.wait_recv()
     f_send[...] = (f_part[core] + f_in[...]).astype(BF16)
-    f_second = exchange(f_send, f_got, 3, across)
+    f_second = exchange(f_send, f_got, 10, across)
+    m_third.append(m_back(1))
+
+    m_third.append(m_back(2))
 
     for c in range(3):
         mirror = -1.0 if c == 1 else 1.0
@@ -480,13 +491,9 @@
     )
     body.start()
 
-    m_second.wait_recv()
-    m_tot[core] = m_send[...].astype(F32) + m_got[...].astype(F32)
-    m_third = exchange(m_tot.at[core], m_tot.at[core], 4, twin)
-
     f_second.wait_recv()
     f_tot[core] = f_send[...].astype(F32) + f_got[...].astype(F32)
-    f_third = exchange(f_tot.at[core], f_tot.at[core], 5, twin)
+    f_third = exchange(f_tot.at[core], f_tot.at[core], 11, twin)
 
     everyone = pl.ds(0, les_size - 1)
     pltpu.make_async_copy(r0.at[everyone], r3.at[everyone], r_recv).wait()
@@ -514,7 +521,8 @@
     for copy in rims:
         copy.start()
 
-    m_third.wait_recv()
+    for copy in m_third:
+        copy.wait_recv()
     gm_copy = pltpu.make_async_copy(m_tot, gm_hbm, local_sem.at[6])
     gm_copy.start()
     f_third.wait_recv()
@@ -534,26 +542,24 @@
         copy.wait()
 
 
-def hand_on(*refs):
-    count = (len(refs) - 2) // 3
-    given, results, held = refs[:count], refs[count : 2 * count], refs[2 * count : 3 * count]
-    into, out = refs[-2:]
-    parts = [(i, k) for i in range(count) for k in range(given[i].shape[0] if given[i].shape[0] == 3 else 1)]
-
-    def pick(ref, k):
-        return ref.at[k] if ref.shape[0] == 3 else ref
-
-    loads = [
-        pltpu.make_async_copy(pick(given[i], k), pick(held[i], k), into.at[n]) for n, (i, k) in enumerate(parts)
-    ]
-    stores = [
-        pltpu.make_async_copy(pick(held[i], k), pick(results[i], k), out.at[n]) for n, (i, k) in enumerate(parts)
-    ]
+def hand_on(ws, go, nv, gf, gm, ws_out, go_out, nv_out, gf_out, gm_out, ws_v, go_v, nv_v, gf_v, gm_v, into, out):
+    moves = [((nv.at[c], nv_v.at[c]), [(nv_v.at[c], nv_out.at[c])]) for c in range(3)]
+    for d in range(3):
+        taps = [
+            (gm_v.at[d, pl.ds(k * C, C)], gm_out.at[pl.ds((3 * k + d) * C, C)]) for k in range(3)
+        ]
+        moves.append(((gm.at[d], gm_v.at[d]), taps))
+    moves += [((gf, gf_v), [(gf_v, gf_out)]), ((ws, ws_v), [(ws_v, ws_out)]), ((go, go_v), [(go_v, go_out)])]
+    loads = [pltpu.make_async_copy(*load, into.at[n]) for n, (load, _) in enumerate(moves)]
     for load in loads:
         load.start()
-    for load, store in zip(loads, stores):
+    stores = []
+    for load, (_, parts) in zip(loads, moves):
         load.wait()
-        store.start()
+        for part in parts:
+            store = pltpu.make_async_copy(*part, out.at[len(stores)])
+            store.start()
+            stores.append(store)
     for store in stores:
         store.wait()
 
@@ -566,7 +572,7 @@
     _, _, ny, cx = velocity.shape
     tiles = owner_map.shape[0]
     hidden = TX * CZ * C
-    half_m, half_f = 9 * C // 2, 224
+    share, half_f = 3 * C // 2, 224
     yl = min(128, ny)
     vmem = pltpu.VMEM
     scratch = [
@@ -591,10 +597,10 @@
         vmem((qn, CAP * zn, DATA), BF16),
         vmem((zn, CAP * qn, DATA), BF16),
         vmem((zn, CAP * qn, DATA), BF16),
-        vmem((qn, CAP * zn, PRED), BF16),
-        vmem((qn, CAP * zn, PRED), BF16),
-        vmem((zn, CAP * qn, PRED), BF16),
-        vmem((zn, CAP * qn, PRED), BF16),
+        vmem((qn, CAP * zn, MORE), BF16),
+        vmem((qn, CAP * zn, MORE), BF16),
+        vmem((zn, CAP * qn, MORE), BF16),
+        vmem((zn, CAP * qn, MORE), BF16),
         vmem((les_size, 1, PRED), F32),
         vmem((les_size, 1, PRED), F32),
         vmem((CZ, 3, ny, cx), BF16),
@@ -608,11 +614,11 @@
         vmem((rows, hidden), F32),
         vmem((rows, hidden), F32),
         vmem((rows, hidden), BF16),
-        vmem((2, half_m, C), F32),
-        vmem((half_m, C), F32),
-        vmem((half_m, C), BF16),
-        vmem((half_m, C), BF16),
-        vmem((2, half_m, C), F32),
+        vmem((3, 2 * share, C), F32),
+        vmem((3, share, C), F32),
+        vmem((3, share, C), BF16),
+        vmem((3, share, C), BF16),
+        vmem((3, 2 * share, C), F32),
         vmem((2, half_f, C), F32),
         vmem((half_f, C), F32),
         vmem((half_f, C), BF16),
@@ -631,8 +637,8 @@
         pltpu.SemaphoreType.DMA(()),
         pltpu.SemaphoreType.DMA((4,)),
         pltpu.SemaphoreType.DMA((4,)),
-        pltpu.SemaphoreType.DMA((6,)),
-        pltpu.SemaphoreType.DMA((6,)),
+        pltpu.SemaphoreType.DMA((12,)),
+        pltpu.SemaphoreType.DMA((12,)),
     ]
     anywhere = pl.BlockSpec(memory_space=pl.ANY)
     shapes = (
@@ -640,7 +646,7 @@
         jax.ShapeDtypeStruct((2, C), F32),
         jax.ShapeDtypeStruct(velocity.shape, F32),
         jax.ShapeDtypeStruct((9 * CIN, C), F32),
-        jax.ShapeDtypeStruct((2, half_m, C), F32),
+        jax.ShapeDtypeStruct((3, 3 * C, C), F32),
     )
     results = pl.pallas_call(
         kernel,
@@ -662,18 +668,18 @@
     )
     stress, grad_out, new_velocity, grad_first, grad_mid = pl.pallas_call(
         hand_on,
-        out_shape=shapes,
+        out_shape=shapes[:4] + (jax.ShapeDtypeStruct((9 * C, C), F32),),
         in_specs=[anywhere] * 5,
         out_specs=(anywhere,) * 5,
         scratch_shapes=[pltpu.VMEM(s.shape, s.dtype) for s in shapes]
-        + [pltpu.SemaphoreType.DMA((7,)), pltpu.SemaphoreType.DMA((7,))],
+        + [pltpu.SemaphoreType.DMA((9,)), pltpu.SemaphoreType.DMA((15,))],
         compiler_params=pltpu.CompilerParams(vmem_limit_bytes=60 * 2**20),
     )(*results)
     return (
         new_velocity,
         stress.transpose(0, 1, 3, 2),
         grad_first[None],
-        grad_mid.reshape(1, 9 * C, C),
+        grad_mid[None],
         grad_out.T[None],
     )
 

time: 52.8 us -> 52.9 us (level)
  no operation moved by 1% of the time
where the time goes in v4:
time: 52.9 us; the launch traced here: 52.8 us
  Pallas kernels  52.1 us (98%)
  between operations  0.64 us (1%)
    pallas_call x1, Pallas kernels, per_device(): pl.pallas_call(kernel, out_shape=shapes, in_specs=[anywhere] * 7, out_spe...  49.8 us
    pallas_call x1, Pallas kernels, per_device(): pl.pallas_call(hand_on, out_shape=shapes[:4] + (jax.ShapeDtypeStruct((9 *...  2.3 us

profile of v4, /device:TPU:1, one launch (start us, length us, event | category | flops | bytes accessed | tf_op | source)
XLA Modules:
  0.0 52.8 jit_solution(9616174928498340310)
XLA Ops:
  0.6 49.8 %shard_map.110 = (f32[2,2,2,128]{3,2,1,0:T(2,128)}, f32[2,128]{1,0:T(2,128)}, f32[3,2,256,128]{3,2,1,0:T(8,128)}, f32[432,128]{1,0:T(8,128)}, f32[3,384,128]{2,1,0:T(8,128)}) custom-call(s32[1,64]{1,0:T(1,128)} %bitcast.16, s32[1,64]{1,0:T(1,128)} %ord_hbm.1, bf16[2,2,2,128]{3,2,1,0:T(2,128)(2,1)} %bitcast.15, bf16[2,128]{1,0:T(2,128)(2,1)} %bitcast.17, ...), custom_call_target="tpu_custom_call" | custom-call | tf_op jit(solution)/shard_map/pallas_call | solution.py:651
  50.5 2.3 %shard_map.111 = (f32[2,2,2,128]{3,2,1,0:T(2,128)}, f32[2,128]{1,0:T(2,128)}, f32[3,2,256,128]{3,2,1,0:T(8,128)}, f32[432,128]{1,0:T(8,128)}, f32[1152,128]{1,0:T(8,128)}) custom-call(f32[2,2,2,128]{3,2,1,0:T(2,128)} %get-tuple-element.15.ws, f32[2,128]{1,0:T(2,128)} %get-tuple-element.16.go, f32[3,2,256,128]{3,2,1,0:T(8,128)} %get-tuple-element.17.nv, ...), custom_call_target="tpu_custom_call" | custom-call | tf_op jit(solution)/shard_map/pallas_call | solution.py:669
